TPU v7x, 256 devices: a whole 4x4x8 slice. The times are simulated.
256 devices in a mesh: lat: 4 (over y_lo, core), lon: 64 (over z, y_hi, x).
Axes of the slice: x: 4, y: 4 (y_hi: 2, y_lo: 2; y = y_hi * 2 + y_lo), z: 8, core: 2. Of those that a mesh axis runs over, the one named last changes fastest.
Arguments:
- inputs: bfloat16 [2, 192, 768, 512], P(None, 'lat', 'lon'), may hold values from -16 to 16
- cotangent: bfloat16 [2, 192, 768, 512], P(None, 'lat', 'lon'), may hold values from -16 to 16
- w_qkv: bfloat16 [512, 1536], replicated, may hold values from -0.25 to 0.25
- w_out: bfloat16 [512, 512], replicated, may hold values from -0.25 to 0.25
- gain: float32 [512], replicated, may hold values from 0.5 to 1.5
- logit_scale: float32 [16], replicated, may hold values from 2 to 12
Outputs:
- out: bfloat16 [2, 192, 768, 512], P(None, 'lat', 'lon')
- grad_in: bfloat16 [2, 192, 768, 512], P(None, 'lat', 'lon')
- grad_qkv: float32 [512, 1536], P('lon')
- grad_out: float32 [512, 512], P(None, 'lon')
All inputs are finite; a program needn't handle non-finite values.
Results may differ from a plain program's by a relative error of at most 0.017.
Values may be sent and summed in bfloat16 or wider, within the bound.
A program may use at most 128 MiB of HBM per device.

v0:
```python
import jax
import jax.numpy as jnp
from jax import lax
from jax.sharding import PartitionSpec as P

HEADS = 16
WIN_LAT = 6
WIN_LON = 12
SHIFT_LAT = 3
SHIFT_LON = 6


norm_floor = 1e-06
norm_eps = 1e-05


def from_behind(value, axis, steps):
    count = lax.axis_size(axis)
    pairs = [(source, (source + steps) % count) for source in range(count)]
    return lax.ppermute(value, axis, pairs)


def to_windows(grid):
    levels, height, breadth, depth = grid.shape
    blocks = grid.reshape(levels, height // WIN_LAT, WIN_LAT, breadth // WIN_LON, WIN_LON, depth)
    blocks = blocks.transpose(1, 3, 0, 2, 4, 5)
    return blocks.reshape(-1, levels * WIN_LAT * WIN_LON, depth)


def from_windows(windows, levels, height, breadth):
    depth = windows.shape[-1]
    blocks = windows.reshape(height // WIN_LAT, breadth // WIN_LON, levels, WIN_LAT, WIN_LON, depth)
    return blocks.transpose(2, 0, 3, 1, 4, 5).reshape(levels, height, breadth, depth)


def window_pass(x_win, g_win, flag_win, keep_win, w_qkv, w_out, gain, logit_scale):
    tokens, width = x_win.shape
    head_size = width // HEADS
    qkv = jnp.dot(x_win, w_qkv, preferred_element_type=jnp.float32).astype(jnp.bfloat16)
    split = qkv.reshape(tokens, 3, HEADS, head_size)
    query = split[:, 0].astype(jnp.float32)
    key_part = split[:, 1].astype(jnp.float32)
    value_b = split[:, 2]
    q_length = jnp.sqrt(jnp.sum(query * query, -1, keepdims=True))
    k_length = jnp.sqrt(jnp.sum(key_part * key_part, -1, keepdims=True))
    q_radius = jnp.maximum(q_length, norm_floor)
    k_radius = jnp.maximum(k_length, norm_floor)
    unit_q = (query / q_radius).astype(jnp.bfloat16)
    unit_k = (key_part / k_radius).astype(jnp.bfloat16)
    scores = (
        jnp.einsum("ihd,jhd->hij", unit_q, unit_k, preferred_element_type=jnp.float32)
        * logit_scale[:, None, None]
    )
    allowed = flag_win[:, None] == flag_win[None, :]
    expo = jnp.where(allowed[None], jnp.exp(scores), jnp.zeros_like(scores))
    probs = expo / jnp.sum(expo, -1, keepdims=True)
    probs_b = probs.astype(jnp.bfloat16)
    attended = jnp.einsum("hij,jhd->ihd", probs_b, value_b, preferred_element_type=jnp.float32)
    attended = attended.reshape(tokens, width).astype(jnp.bfloat16)
    projected = jnp.dot(attended, w_out, preferred_element_type=jnp.float32)
    centre = jnp.mean(projected, -1, keepdims=True)
    spread_sq = jnp.mean((projected - centre) ** 2, -1, keepdims=True)
    inverse = lax.rsqrt(spread_sq + norm_eps)
    normed = (projected - centre) * inverse
    branch = (gain * normed).astype(jnp.bfloat16)
    upstream = gain * g_win.astype(jnp.float32)
    dproj = (
        upstream
        - jnp.mean(upstream, -1, keepdims=True)
        - normed * jnp.mean(upstream * normed, -1, keepdims=True)
    ) * inverse
    dproj_b = dproj.astype(jnp.bfloat16)
    keep_b = keep_win.astype(jnp.bfloat16)[:, None]
    grad_out = jnp.dot((attended * keep_b).T, dproj_b, preferred_element_type=jnp.float32)
    dattended = jnp.dot(dproj_b, w_out.T, preferred_element_type=jnp.float32).astype(jnp.bfloat16)
    dattended = dattended.reshape(tokens, HEADS, head_size)
    dprobs = jnp.einsum("ihd,jhd->hij", dattended, value_b, preferred_element_type=jnp.float32)
    dvalue = jnp.einsum("hij,ihd->jhd", probs_b, dattended, preferred_element_type=jnp.float32)
    dscores = (probs * (dprobs - jnp.sum(probs * dprobs, -1, keepdims=True))).astype(jnp.bfloat16)
    dunit_q = (
        jnp.einsum("hij,jhd->ihd", dscores, unit_k, preferred_element_type=jnp.float32)
        * logit_scale[None, :, None]
    )
    dunit_k = (
        jnp.einsum("hij,ihd->jhd", dscores, unit_q, preferred_element_type=jnp.float32)
        * logit_scale[None, :, None]
    )
    q_tail = jnp.where(
        q_length > norm_floor,
        query * jnp.sum(query * dunit_q, -1, keepdims=True) / q_radius**3,
        jnp.zeros_like(query),
    )
    k_tail = jnp.where(
        k_length > norm_floor,
        key_part * jnp.sum(key_part * dunit_k, -1, keepdims=True) / k_radius**3,
        jnp.zeros_like(key_part),
    )
    grad_q = dunit_q / q_radius - q_tail
    grad_k = dunit_k / k_radius - k_tail
    dqkv = (
        jnp.stack([grad_q, grad_k, dvalue], axis=1).reshape(tokens, 3 * width).astype(jnp.bfloat16)
    )
    dshifted = jnp.dot(dqkv, w_qkv.T, preferred_element_type=jnp.float32).astype(jnp.bfloat16)
    grad_qkv = jnp.dot((x_win * keep_b).T, dqkv, preferred_element_type=jnp.float32)
    return (branch, dshifted, grad_qkv, grad_out)


def run_windows(x_grid, g_grid, flag_grid, keep_grid, w_qkv, w_out, gain, logit_scale):
    levels, height, breadth, width = x_grid.shape

    def visit(totals, window_item):
        branch, dshifted, grad_qkv, grad_out = window_pass(
            window_item[0],
            window_item[1],
            window_item[2],
            window_item[3],
            w_qkv,
            w_out,
            gain,
            logit_scale,
        )
        return ((totals[0] + grad_qkv, totals[1] + grad_out), (branch, dshifted))

    start = (jnp.zeros(w_qkv.shape, jnp.float32), jnp.zeros(w_out.shape, jnp.float32))
    windows = (
        to_windows(x_grid),
        to_windows(g_grid),
        to_windows(flag_grid)[:, :, 0],
        to_windows(keep_grid)[:, :, 0],
    )
    totals, stacked = lax.scan(visit, start, windows)
    branch = from_windows(stacked[0], levels, height, breadth)
    dshifted = from_windows(stacked[1], levels, height, breadth)
    return (branch, dshifted, totals[0], totals[1])


def body(inputs, cotangent, w_qkv, w_out, gain, logit_scale):
    levels, tile_rows, tile_cols, width = inputs.shape
    lat_first = lax.axis_index("lat") * tile_rows
    total_lat = tile_rows * lax.axis_size("lat")
    top_rows = (inputs[:, :SHIFT_LAT], cotangent[:, :SHIFT_LAT])
    below = from_behind((top_rows[0], top_rows[1]), "lat", -1)
    ext_x = jnp.concatenate([inputs[:, SHIFT_LAT:], below[0]], axis=1)
    ext_g = jnp.concatenate([cotangent[:, SHIFT_LAT:], below[1]], axis=1)
    beside = from_behind((ext_x[:, :, :SHIFT_LON], ext_g[:, :, :SHIFT_LON]), "lon", -1)
    shifted = jnp.concatenate([ext_x[:, :, SHIFT_LON:], beside[0]], axis=2)
    shifted_cot = jnp.concatenate([ext_g[:, :, SHIFT_LON:], beside[1]], axis=2)
    anchor = (lat_first + jnp.arange(tile_rows, dtype=jnp.int32) + SHIFT_LAT) % total_lat
    flags = (anchor < SHIFT_LAT).astype(jnp.int32)
    flag_grid = jnp.broadcast_to(flags[None, :, None, None], (levels, tile_rows, tile_cols, 1))
    keep_grid = jnp.ones((levels, tile_rows, tile_cols, 1), jnp.float32)
    branch, dshifted, grad_qkv, grad_out = run_windows(
        shifted, shifted_cot, flag_grid, keep_grid, w_qkv, w_out, gain, logit_scale
    )
    tail_cols = (branch[:, :, tile_cols - SHIFT_LON :], dshifted[:, :, tile_cols - SHIFT_LON :])
    came_cols = from_behind((tail_cols[0], tail_cols[1]), "lon", 1)
    part_branch = jnp.concatenate([came_cols[0], branch[:, :, : tile_cols - SHIFT_LON]], axis=2)
    part_grad = jnp.concatenate([came_cols[1], dshifted[:, :, : tile_cols - SHIFT_LON]], axis=2)
    tail_rows = (part_branch[:, tile_rows - SHIFT_LAT :], part_grad[:, tile_rows - SHIFT_LAT :])
    came_rows = from_behind((tail_rows[0], tail_rows[1]), "lat", 1)
    branch_own = jnp.concatenate([came_rows[0], part_branch[:, : tile_rows - SHIFT_LAT]], axis=1)
    dshift_own = jnp.concatenate([came_rows[1], part_grad[:, : tile_rows - SHIFT_LAT]], axis=1)
    out = (inputs.astype(jnp.float32) + branch_own.astype(jnp.float32)).astype(jnp.bfloat16)
    grad_in = (cotangent.astype(jnp.float32) + dshift_own.astype(jnp.float32)).astype(jnp.bfloat16)
    summed = (
        lax.psum(grad_qkv.astype(jnp.bfloat16), "lat").astype(jnp.float32),
        lax.psum(grad_out.astype(jnp.bfloat16), "lat").astype(jnp.float32),
    )
    share_qkv, share_out = (
        lax.psum_scatter(summed[0], "lon", scatter_dimension=0, tiled=True),
        lax.psum_scatter(summed[1], "lon", scatter_dimension=1, tiled=True),
    )
    return (out, grad_in, share_qkv, share_out)


def solution(mesh):
    placed = (P(None, "lat", "lon", None), P(None, "lat", "lon", None), P(), P(), P(), P())
    return jax.shard_map(
        body,
        mesh=mesh,
        in_specs=placed,
        out_specs=(
            P(None, "lat", "lon", None),
            P(None, "lat", "lon", None),
            P("lon", None),
            P(None, "lon"),
        ),
        check_vma=False,
    )
```

profile of v0, /device:TPU:1, one launch (start us, length us, event | category | flops | bytes accessed | tf_op | source)
XLA Modules:
  0.0 1500.7 jit_solution(12198195555495036450)
XLA Ops:
  8.2 3.3 collective-permute-start
  14.6 9.4 collective-permute-start.1
  27.5 8.5 collective-permute-done.1
  39.4 9.2 collective-permute-done.3
  52.6 221.1 %while.19 = (s32[]{:T(128)}, f32[512,1536]{1,0:T(8,128)}, f32[512,512]{1,0:T(8,128)}, bf16[8,144,512]{2,1,0:T(8,128)(2,1)}, bf16[8,144,512]{2,1,0:T(8,128)(2,1)}...) while((s32[]{:T(128)}, f32[512,1536]{1,0:T(8,128)}, ...), condition=%wide.region_11.12_spmd.clone, body=%wide.region_0.11_spmd.clone.sunk | while | flops 1048922048 | bytes 85576072 | solution.py:131
  64.6 2.4 convolution_bitcast_fusion.2
  76.0 2.5 convolution_add_fusion.4
  92.2 2.4 convolution_bitcast_fusion.2
  103.7 2.5 convolution_add_fusion.4
  119.8 2.4 convolution_bitcast_fusion.2
  131.3 2.5 convolution_add_fusion.4
  147.4 2.4 convolution_bitcast_fusion.2
  158.9 2.5 convolution_add_fusion.4
  175.1 2.4 convolution_bitcast_fusion.2
  186.5 2.5 convolution_add_fusion.4
  214.2 2.5 convolution_add_fusion.4
  241.8 2.5 convolution_add_fusion.4
  269.5 2.5 convolution_add_fusion.4
  275.9 3.2 convert_element_type.161
  279.2 63.1 %all-reduce.3.cloned.1.call-done = (bf16[512,1536]{1,0:T(8,128)(2,1)}, bf16[512,512]{0,1:T(8,128)(2,1)}) async-done(((bf16[512,1536]{1,0:T(8,128)(2,1)}, bf16[512,512]{0,1:T(8,128)(2,1)}), (bf16[512,1536]{1,0:T(8,128)(2,1)}, bf16[512,512]{0,1:T(8,128)(2,1)})) %all-reduce.3.cloned.1.call-update) | async-done | bytes 2097168 | tf_op jit(solution)/shard_map/psum | solution.py:166
  356.1 15.8 %collective-permute-done.6 = bf16[2,48,6,512]{3,0,2,1:T(2,128)(2,1)S(1)} collective-permute-done((bf16[2,48,6,512]{3,0,2,1:T(2,128)(2,1)S(1)}, bf16[2,48,6,512]{3,0,2,1:T(2,128)(2,1)S(1)}, u32[]{:S(2)}, u32[]{:S(2)}) %collective-permute-start.6) | collective-permute-done | bytes 589856 | tf_op jit(solution)/shard_map/ppermute | solution.py:20
  373.4 11.5 collective-permute-done.4
  392.0 267.1 %reduce-scatter.5.cloned.1.call-done = f32[512,8]{0,1:T(8,128)} async-done(((f32[512,512]{0,1:T(8,128)}), f32[512,8]{0,1:T(8,128)}) %reduce-scatter.5.cloned.1.call-update) | async-done | bytes 16400 | tf_op jit(solution)/shard_map/reduce_scatter | solution.py:171
  659.1 835.1 %reduce-scatter.3.cloned.1.call-done = f32[8,1536]{1,0:T(8,128)} async-done(((f32[512,1536]{1,0:T(8,128)}), f32[8,1536]{1,0:T(8,128)}) %reduce-scatter.3.cloned.1.call-update) | async-done | bytes 49168 | tf_op jit(solution)/shard_map/reduce_scatter | solution.py:170
  (587 shorter events, 226.3 us)
Async XLA Ops:
  7.2 335.1 %all-reduce.3.cloned.1.call-start = ((), (), s32[]{:S(2)}) async-start(), calls=%async_computation.4 | async-start | bytes 4194304 | tf_op jit(solution)/shard_map/psum | solution.py:166
  8.2 6.2 collective-permute-start
  12.4 12.1 collective-permute-start.2
  14.4 9.6 copy-start.9
  14.6 21.4 %collective-permute-start.1 = (bf16[2,48,6,512]{3,1,2,0:T(8,128)(2,1)S(1)}, bf16[2,48,6,512]{3,1,2,0:T(8,128)(2,1)S(1)}, u32[]{:S(2)}, u32[]{:S(2)}) collective-permute-start(bf16[2,48,6,512]{3,1,2,0:T(8,128)(2,1)S(1)} %get-tuple-element.262), channel_id=1, source_target_pairs={{0,63},{1,0},{2,1},{3,2},{4,3},{5,4},{6,5},{7,6},{8,7},{9,8},{10,9... | collective-permute-start | bytes 1769480 | tf_op jit(solution)/shard_map/ppermute | solution.py:20
  24.7 23.9 %collective-permute-start.3 = (bf16[2,48,6,512]{3,1,2,0:T(8,128)(2,1)S(1)}, bf16[2,48,6,512]{3,1,2,0:T(8,128)(2,1)S(1)}, u32[]{:S(2)}, u32[]{:S(2)}) collective-permute-start(bf16[2,48,6,512]{3,1,2,0:T(8,128)(2,1)S(1)} %get-tuple-element.260), channel_id=1, source_target_pairs={{0,63},{1,0},{2,1},{3,2},{4,3},{5,4},{6,5},{7,6},{8,7},{9,8},{10,9... | collective-permute-start | bytes 1769480 | tf_op jit(solution)/shard_map/ppermute | solution.py:20
  76.0 4.2 copy-start.24
  76.0 4.2 copy-start.27
  103.7 4.2 copy-start.27
  131.3 4.2 copy-start.24
  131.3 4.2 copy-start.27
  158.9 4.2 copy-start.24
  158.9 4.2 copy-start.27
  186.5 4.2 copy-start.27
  214.2 4.2 copy-start.27
  241.8 4.2 copy-start.27
  269.4 4.2 copy-start.27
  279.1 380.0 %reduce-scatter.5.cloned.1.call-start = ((), (), s32[]{:S(2)}) async-start(), calls=%async_computation.3 | async-start | bytes 1064960 | tf_op jit(solution)/shard_map/reduce_scatter | solution.py:171
  344.6 1149.6 %reduce-scatter.3.cloned.1.call-start = ((), (), s32[]{:S(2)}) async-start(), calls=%async_computation.2 | async-start | bytes 3194880 | tf_op jit(solution)/shard_map/reduce_scatter | solution.py:170
  350.9 21.0 %collective-permute-start.6 = (bf16[2,48,6,512]{3,0,2,1:T(2,128)(2,1)S(1)}, bf16[2,48,6,512]{3,0,2,1:T(2,128)(2,1)S(1)}, u32[]{:S(2)}, u32[]{:S(2)}) collective-permute-start(bf16[2,48,6,512]{3,0,2,1:T(2,128)(2,1)S(1)} %get-tuple-element.263), channel_id=1, source_target_pairs={{0,1},{1,2},{2,3},{3,4},{4,5},{5,6},{6,7},{7,8},{8,9},{9,10},{10,1... | collective-permute-start | bytes 1769480 | tf_op jit(solution)/shard_map/ppermute | solution.py:20
  354.9 30.0 %collective-permute-start.4 = (bf16[2,48,6,512]{3,0,2,1:T(2,128)(2,1)S(1)}, bf16[2,48,6,512]{3,0,2,1:T(2,128)(2,1)S(1)}, u32[]{:S(2)}, u32[]{:S(2)}) collective-permute-start(bf16[2,48,6,512]{3,0,2,1:T(2,128)(2,1)S(1)} %get-tuple-element.265), channel_id=1, source_target_pairs={{0,1},{1,2},{2,3},{3,4},{4,5},{5,6},{6,7},{7,8},{8,9},{9,10},{10,1... | collective-permute-start | bytes 1769480 | tf_op jit(solution)/shard_map/ppermute | solution.py:20
  371.9 14.3 copy-start.10
  372.0 14.2 collective-permute-start.7
  385.0 4.1 collective-permute-start.5
  (141 other events, 251.0 us)
Sparse Core Ops, SparseCore 0:
  279.2 62.9 all-reduce.2
  345.5 313.5 reduce-scatter.4
  665.3 828.8 reduce-scatter.2
where the time goes:
time: 1510 us; the launch traced here: 1500 us
  waiting for transfers between devices  1210 us (80%)
  matrix products  124 us (8%)
  local copies, waits for them, and re-layouts  78.4 us (5%)
  other arithmetic  53.2 us (4%)
  starting transfers between devices  19.4 us (1%)
    reduce_scatter x1, waiting for transfers between devices, body(): lax.psum_scatter(summed[0], 'lon', scatter_dimension=0, tiled=True)  835 us
    reduce_scatter x1, waiting for transfers between devices, body(): lax.psum_scatter(summed[1], 'lon', scatter_dimension=1, tiled=True)  267 us
    psum x1, waiting for transfers between devices, body(): lax.psum(grad_qkv.astype(jnp.bfloat16), 'lat').astype(jnp.float32)  63.1 us
    ppermute x8, waiting for transfers between devices, from_behind(): return lax.ppermute(value, axis, pairs)  45 us
    while x288, local copies, waits for them, and re-layouts  37.5 us
  transfers between devices with their start and end apart: 11, of which 7 were waited for; matrix products, arithmetic and copies ran while one was open for 1% of the time, Pallas kernels for 0%

commit v1 on v0

v1 whole, which is shorter than its diff:
```python
import functools

import jax
import jax.numpy as jnp
from jax import lax
from jax.experimental import pallas as pl
from jax.experimental.pallas import tpu as pltpu
from jax.sharding import PartitionSpec as P

BF = jnp.bfloat16
F32 = jnp.float32
MESH = pl.DeviceIdType.MESH
HEADS = 16
WIDTH = 512
HALF = 72
TOK = 144
QUART = 36
KEYS = 8 * TOK
LOG2E = 1.4426950408889634
FLOOR = 1e-6
EPS = 1e-5


def nn(a, b):
    return jnp.dot(a, b, preferred_element_type=F32)


def nt(a, b):
    return lax.dot_general(a, b, (((1,), (1,)), ((), ())), preferred_element_type=F32)


def tn(a, b):
    return lax.dot_general(a, b, (((0,), (0,)), ((), ())), preferred_element_type=F32)


def spread(part):
    head = lax.broadcasted_iota(jnp.int32, part.shape, 1) // 32
    zero = jnp.zeros_like(part)
    return jnp.concatenate([jnp.where(head == h, part, zero) for h in range(8)], axis=0)


def head_sum(value, ones_block):
    return nn(value.astype(BF), ones_block)


def head_sum_fine(value, ones_block):
    high = value.astype(BF)
    low = (value - high.astype(F32)).astype(BF)
    return nn(high, ones_block) + nn(low, ones_block)


def window_math(xw, gw, split, w_qkv, w_out, gain, scale_cols, scale_lanes, ones_big, ones_blk, qkv):
    qkv[...] = nn(xw, w_qkv[...]).astype(BF)
    ones_block = ones_blk[...]
    row = lax.broadcasted_iota(jnp.int32, (TOK, 1), 0)
    col = lax.broadcasted_iota(jnp.int32, (1, KEYS), 1)
    row_flag = jnp.where(split, (row // QUART) % 2, 0)
    col_flag = jnp.where(split, (col // QUART) % 2, 0)
    allowed = row_flag == col_flag
    att = []
    saved = []
    for half in range(2):
        lo = half * 256
        q = qkv[:, lo : lo + 256].astype(F32)
        k = qkv[:, 512 + lo : 768 + lo].astype(F32)
        v = qkv[:, 1024 + lo : 1280 + lo]
        q_len = jnp.sqrt(head_sum_fine(q * q, ones_block))
        k_len = jnp.sqrt(head_sum_fine(k * k, ones_block))
        q_inv = 1.0 / jnp.maximum(q_len, FLOOR)
        k_inv = 1.0 / jnp.maximum(k_len, FLOOR)
        uq = (q * q_inv).astype(BF)
        uk = (k * k_inv).astype(BF)
        scl = scale_cols[half : half + 1, :]
        k_big = spread(uk)
        e = jnp.exp2(nt(uq, k_big) * scl)
        e = jnp.where(allowed, e, 0.0).astype(BF)
        v_big = spread(v)
        r_den = 1.0 / nn(e, ones_big[...])
        att.append((nn(e, v_big) * r_den).astype(BF))
        saved.append((q, k, v, q_len, k_len, q_inv, k_inv, uq, uk, k_big, v_big, e, r_den, scl))
    att_b = jnp.concatenate(att, axis=1)
    proj = nn(att_b, w_out[...])
    dev = proj - jnp.mean(proj, -1, keepdims=True)
    inv = lax.rsqrt(jnp.mean(dev * dev, -1, keepdims=True) + EPS)
    normed = dev * inv
    branch = gain * normed
    up = gain * gw
    dproj = (
        (up - jnp.mean(up, -1, keepdims=True) - normed * jnp.mean(up * normed, -1, keepdims=True))
        * inv
    ).astype(BF)
    datt = nt(dproj, w_out[...]).astype(BF)
    dq, dk, dv = [], [], []
    for half in range(2):
        lo = half * 256
        q, k, v, q_len, k_len, q_inv, k_inv, uq, uk, k_big, v_big, e, r_den, scl = saved[half]
        dh = datt[:, lo : lo + 256].astype(F32) * r_den
        dh_b = dh.astype(BF)
        dd = (dh * att[half].astype(F32)).astype(BF)
        t = nt(dh_b, v_big) - nt(dd, ones_big[...])
        ds = (e.astype(F32) * t).astype(BF)
        lanes = scale_lanes[half : half + 1, :]
        duq = nn(ds, k_big) * lanes
        q_big = spread(uq)
        et = jnp.exp2(nt(uk, q_big) * scl)
        et = jnp.where(allowed, et, 0.0).astype(BF)
        d_big = spread(dh_b)
        dd_big = spread(dd)
        tt = nt(v, d_big) - nt(jnp.ones((TOK, 256), BF), dd_big)
        dst = (et.astype(F32) * tt).astype(BF)
        duk = nn(dst, q_big) * lanes
        qn = q * q_inv
        kn = k * k_inv
        q_tail = jnp.where(q_len > FLOOR, qn * head_sum(qn * duq, ones_block), 0.0)
        k_tail = jnp.where(k_len > FLOOR, kn * head_sum(kn * duk, ones_block), 0.0)
        dq.append(((duq - q_tail) * q_inv).astype(BF))
        dk.append(((duk - k_tail) * k_inv).astype(BF))
        dv.append(nn(et, d_big).astype(BF))
    dqkv = jnp.concatenate(dq + dk + dv, axis=1)
    dshifted = nt(dqkv, w_qkv[...])
    return branch, dshifted, att_b, dproj, dqkv


def pack(ref, rows, first_col):
    parts = []
    for r in rows:
        for lev in range(2):
            parts.append(ref[lev, r].astype(F32)[first_col : first_col + 6])
    return jnp.concatenate(parts, axis=0)


def piece_of(x_part, g_part):
    pad = jnp.zeros((4, WIDTH), F32)
    return jnp.concatenate([x_part, pad, g_part, pad], axis=0).astype(BF)


def unpiece(ref):
    whole = ref.astype(F32)
    return whole[:QUART], whole[40 : 40 + QUART]


def attention_kernel(
    x_ref,
    g_ref,
    w_qkv,
    w_out,
    gain_ref,
    scale_cols,
    scale_lanes,
    ones_big,
    ones_blk,
    out_ref,
    gin_ref,
    grads_ref,
    send,
    recv,
    own,
    back_send,
    back_recv,
    own_res,
    send7,
    recv7,
    back7_send,
    back7_recv,
    qkv,
    x_all,
    att_all,
    dproj_all,
    dqkv_all,
    send_sem,
    recv_sem,
    back_send_sem,
    back_recv_sem,
    send7_sem,
    recv7_sem,
    back7_send_sem,
    back7_recv_sem,
):
    n_lat = lax.axis_size("lat")
    n_lon = lax.axis_size("lon")
    a = lax.axis_index("lat")
    b = lax.axis_index("lon")
    up_a = lax.rem(a + 1, n_lat)
    dn_a = lax.rem(a + n_lat - 1, n_lat)
    up_b = lax.rem(b + 1, n_lon)
    dn_b = lax.rem(b + n_lon - 1, n_lon)

    barrier = pltpu.get_barrier_semaphore()
    for peer in ((a, up_b), (a, dn_b), (up_a, b), (dn_a, b), (up_a, dn_b), (dn_a, up_b)):
        pl.semaphore_signal(barrier, inc=1, device_id=peer, device_id_type=MESH)
    pl.semaphore_wait(barrier, 6)

    def forth(w, peer):
        return pltpu.make_async_remote_copy(
            src_ref=send.at[w],
            dst_ref=recv.at[w],
            send_sem=send_sem.at[w],
            recv_sem=recv_sem.at[w],
            device_id=peer,
            device_id_type=MESH,
        )

    def back(w, peer):
        return pltpu.make_async_remote_copy(
            src_ref=back_send.at[w],
            dst_ref=back_recv.at[w],
            send_sem=back_send_sem.at[w],
            recv_sem=back_recv_sem.at[w],
            device_id=peer,
            device_id_type=MESH,
        )

    def forth7(j):
        return pltpu.make_async_remote_copy(
            src_ref=send7.at[j],
            dst_ref=recv7.at[j],
            send_sem=send7_sem.at[j],
            recv_sem=recv7_sem.at[j],
            device_id=((a, up_b), (dn_a, b), (dn_a, up_b))[j],
            device_id_type=MESH,
        )

    def back7(j):
        return pltpu.make_async_remote_copy(
            src_ref=back7_send.at[j],
            dst_ref=back7_recv.at[j],
            send_sem=back7_send_sem.at[j],
            recv_sem=back7_recv_sem.at[j],
            device_id=((a, dn_b), (up_a, b), (up_a, dn_b))[j],
            device_id_type=MESH,
        )

    def both(w, first_col):
        rows = [6 * w + 3 + i for i in range(6)]
        return jnp.concatenate(
            [pack(x_ref, rows, first_col), pack(g_ref, rows, first_col)], axis=0
        ).astype(BF)

    @pl.loop(0, 4)
    def _(pair):
        w = 2 * pair
        send[w] = both(w, 0)
        forth(w, (a, dn_b)).start()

        @pl.when(pair < 3)
        def _():
            send[w + 1] = both(w + 1, 6)
            forth(w + 1, (a, up_b)).start()

    low_rows = [45, 46, 47]
    top_rows = [0, 1, 2]
    for j, (rows, first_col) in enumerate(((low_rows, 6), (top_rows, 0), (top_rows, 6))):
        send7[j] = piece_of(pack(x_ref, rows, first_col), pack(g_ref, rows, first_col))
        forth7(j).start()

    @pl.loop(0, 4)
    def _(pair):
        w = 2 * pair
        own[w] = both(w, 6)

        @pl.when(pair < 3)
        def _():
            own[w + 1] = both(w + 1, 0)

    @pl.loop(0, 8)
    def _(w):
        @pl.when(w < 7)
        def _():
            forth(w, (a, up_b)).wait_recv()

        @pl.when(w == 7)
        def _():
            for j in range(3):
                forth7(j).wait_recv()
            low_x = pack(x_ref, low_rows, 0)
            low_g = pack(g_ref, low_rows, 0)
            side_x, side_g = unpiece(recv7[0])
            down_x, down_g = unpiece(recv7[1])
            diag_x, diag_g = unpiece(recv7[2])
            own[7] = jnp.concatenate([low_x, down_x, low_g, down_g], axis=0).astype(BF)
            recv[7] = jnp.concatenate([side_x, diag_x, side_g, diag_g], axis=0).astype(BF)

        mine = own[w].astype(F32)
        theirs = recv[w].astype(F32)
        xw = jnp.concatenate([mine[:HALF], theirs[:HALF]], axis=0).astype(BF)
        gw = jnp.concatenate([mine[HALF:], theirs[HALF:]], axis=0)
        split = jnp.logical_and(w == 7, a == n_lat - 1)
        branch, dshifted, att, dproj, dqkv = window_math(
            xw, gw, split, w_qkv, w_out, gain_ref[...], scale_cols, scale_lanes, ones_big, ones_blk, qkv
        )
        own_res[w] = jnp.concatenate([branch[:HALF], dshifted[:HALF]], axis=0).astype(BF)
        back_send[w] = jnp.concatenate([branch[HALF:], dshifted[HALF:]], axis=0).astype(BF)

        @pl.when(w < 7)
        def _():
            odd = lax.rem(w, 2)
            back(w, (a, up_b * (1 - odd) + dn_b * odd)).start()

        rows = pl.ds(pl.multiple_of(w * TOK, TOK), TOK)
        x_all[rows, :] = xw
        att_all[rows, :] = att
        dproj_all[rows, :] = dproj
        dqkv_all[rows, :] = dqkv

    mine = own_res[7].astype(F32)
    theirs = back_send[7].astype(F32)
    back7_send[0] = piece_of(theirs[:QUART], theirs[HALF : HALF + QUART])
    back7_send[1] = piece_of(mine[QUART:HALF], mine[HALF + QUART :])
    back7_send[2] = piece_of(theirs[QUART:HALF], theirs[HALF + QUART :])
    for j in range(3):
        back7(j).start()

    def column(c):
        if c < 6:
            return tn(x_all[...], dqkv_all[:, c * 256 : (c + 1) * 256])
        return tn(dproj_all[...], att_all[:, (c - 6) * 256 : (c - 5) * 256])

    for part in range(4):
        core, y_lo = part // 2, part % 2
        first = column(part).reshape(64, 8, 256)
        second = column(part + 4).reshape(64, 8, 256)
        joined = jnp.concatenate([first, second], axis=1).astype(BF)
        for lon in range(64):
            z, y, x = lon // 8, 2 * ((lon // 4) % 2) + y_lo, lon % 4
            u, v = (x, y) if core == 0 else (y, x)
            grads_ref[core, u, v, z] = joined[lon]

    def assemble(rows, left_b, right_b, left_d, right_d):
        for i, r in enumerate(rows):
            for lev in range(2):
                at = (2 * i + lev) * 6
                branch = jnp.concatenate([left_b[at : at + 6], right_b[at : at + 6]], axis=0)
                dshift = jnp.concatenate([left_d[at : at + 6], right_d[at : at + 6]], axis=0)
                out_ref[lev, r] = (x_ref[lev, r].astype(F32) + branch).astype(BF)
                gin_ref[lev, r] = (g_ref[lev, r].astype(F32) + dshift).astype(BF)

    @pl.loop(0, 4)
    def _(pair):
        w = 2 * pair
        back(w, (a, up_b)).wait_recv()
        mine = own_res[w].astype(F32)
        came = back_recv[w].astype(F32)
        assemble([6 * w + 3 + i for i in range(6)], came[:HALF], mine[:HALF], came[HALF:], mine[HALF:])

        @pl.when(pair < 3)
        def _():
            v = w + 1
            back(v, (a, up_b)).wait_recv()
            mine = own_res[v].astype(F32)
            came = back_recv[v].astype(F32)
            assemble(
                [6 * v + 3 + i for i in range(6)], mine[:HALF], came[:HALF], mine[HALF:], came[HALF:]
            )

    for j in range(3):
        back7(j).wait_recv()
    mine = own_res[7].astype(F32)
    side_b, side_d = unpiece(back7_recv[0])
    down_b, down_d = unpiece(back7_recv[1])
    diag_b, diag_d = unpiece(back7_recv[2])
    assemble(low_rows, mine[:QUART], side_b, mine[HALF : HALF + QUART], side_d)
    assemble(top_rows, down_b, diag_b, down_d, diag_d)

    @pl.loop(0, 7)
    def _(w):
        forth(w, (a, up_b)).wait_send()
        back(w, (a, up_b)).wait_send()

    for j in range(3):
        forth7(j).wait_send()
        back7(j).wait_send()


def reduce_kernel(
    grads_ref,
    gq_ref,
    go_ref,
    pair_recv,
    mine,
    ring_relay,
    ring_recv,
    cut,
    line_recv,
    piece,
    z_recv,
    part,
    whole,
    pair_send_sem,
    pair_recv_sem,
    relay_send_sem,
    relay_recv_sem,
    ring_send_sem,
    ring_recv_sem,
    line_send_sem,
    line_recv_sem,
    z_send_sem,
    z_recv_sem,
    gather_send_sem,
    gather_recv_sem,
):
    lat = lax.axis_index("lat")
    lon = lax.axis_index("lon")
    core, y_lo = lax.rem(lat, 2), lat // 2
    z, y_hi, x = lon // 8, lax.rem(lon // 4, 2), lax.rem(lon, 4)
    y = 2 * y_hi + y_lo
    u = x * (1 - core) + y * core
    v = y * (1 - core) + x * core
    other_u = y * (1 - core) + x * core

    def device(uu, vv, zz):
        xx = uu * (1 - core) + vv * core
        yy = vv * (1 - core) + uu * core
        return (2 * lax.rem(yy, 2) + core, zz * 8 + (yy // 2) * 4 + xx)

    def mod(value, n):
        return lax.rem(value + n, n)

    partner = (lat + 1 - 2 * core, lon)
    nxt = device(mod(u + 1, 4), v, z)
    prv = device(mod(u + 3, 4), v, z)
    line = [device(u, mod(v + i, 4), z) for i in range(1, 4)]
    column = [device(u, v, mod(z + i, 8)) for i in range(1, 8)]
    group = [(mod(lat + i, 4), lon) for i in range(1, 4)]
    peers = [partner, nxt, prv] + line + column + group
    barrier = pltpu.get_barrier_semaphore()
    for peer in peers:
        pl.semaphore_signal(barrier, inc=1, device_id=peer, device_id_type=MESH)
    pl.semaphore_wait(barrier, len(peers))

    def copy(src, dst, send_sem, recv_sem, peer):
        return pltpu.make_async_remote_copy(
            src_ref=src, dst_ref=dst, send_sem=send_sem, recv_sem=recv_sem, device_id=peer, device_id_type=MESH
        )

    order = (2, 1, 3, 0)
    pair = []
    for i, step in enumerate(order):
        chunk = mod(other_u + step, 4)
        c = copy(
            grads_ref.at[1 - core, chunk],
            pair_recv.at[i],
            pair_send_sem.at[i],
            pair_recv_sem.at[i],
            partner,
        )
        c.start()
        pair.append(c)

    def add_pair(i):
        pair[i].wait_recv()
        chunk = mod(u + order[i], 4)

        @pl.loop(0, 4)
        def _(vv):
            mine[i, vv] = (
                grads_ref[core, chunk, vv].astype(F32) + pair_recv[i, vv].astype(F32)
            ).astype(BF)

    add_pair(0)
    relay_up = copy(mine.at[0, pl.ds(0, 2)], ring_relay.at[0], relay_send_sem.at[0], relay_recv_sem.at[0], nxt)
    relay_dn = copy(mine.at[0, pl.ds(2, 2)], ring_relay.at[1], relay_send_sem.at[1], relay_recv_sem.at[1], prv)
    relay_up.start()
    relay_dn.start()
    add_pair(1)
    up_b = copy(mine.at[1, pl.ds(2, 2)], ring_recv.at[0, pl.ds(2, 2)], ring_send_sem.at[0], ring_recv_sem.at[0], nxt)
    up_b.start()
    add_pair(2)
    dn_a = copy(mine.at[2, pl.ds(0, 2)], ring_recv.at[1, pl.ds(0, 2)], ring_send_sem.at[1], ring_recv_sem.at[1], prv)
    dn_a.start()
    add_pair(3)
    relay_up.wait_recv()

    @pl.loop(0, 2)
    def _(vv):
        mine[1, vv] = (mine[1, vv].astype(F32) + ring_relay[0, vv].astype(F32)).astype(BF)

    up_a = copy(mine.at[1, pl.ds(0, 2)], ring_recv.at[0, pl.ds(0, 2)], ring_send_sem.at[2], ring_recv_sem.at[2], nxt)
    up_a.start()
    relay_dn.wait_recv()

    @pl.loop(0, 2)
    def _(vv):
        mine[2, 2 + vv] = (mine[2, 2 + vv].astype(F32) + ring_relay[1, vv].astype(F32)).astype(BF)

    dn_b = copy(mine.at[2, pl.ds(2, 2)], ring_recv.at[1, pl.ds(2, 2)], ring_send_sem.at[3], ring_recv_sem.at[3], prv)
    dn_b.start()
    for c in (up_b, dn_a, up_a, dn_b):
        c.wait_recv()

    @pl.loop(0, 4)
    def _(vv):
        cut[vv] = (
            mine[3, vv].astype(F32) + ring_recv[0, vv].astype(F32) + ring_recv[1, vv].astype(F32)
        ).astype(BF)

    lines = []
    for i in range(1, 4):
        c = copy(
            cut.at[mod(v + i, 4)], line_recv.at[i - 1], line_send_sem.at[i - 1], line_recv_sem.at[i - 1], line[i - 1]
        )
        c.start()
        lines.append(c)
    for c in lines:
        c.wait_recv()
    piece[...] = (
        cut[v].astype(F32) + line_recv[0].astype(F32) + line_recv[1].astype(F32) + line_recv[2].astype(F32)
    ).astype(BF)
    columns = []
    for i in range(1, 8):
        c = copy(
            piece.at[mod(z + i, 8)], z_recv.at[i - 1], z_send_sem.at[i - 1], z_recv_sem.at[i - 1], column[i - 1]
        )
        c.start()
        columns.append(c)
    for c in columns:
        c.wait_recv()
    total = piece[z].astype(F32)
    for i in range(7):
        total = total + z_recv[i].astype(F32)
    part[...] = total

    here = 2 * core + y_lo
    whole[here] = total
    gathers = []
    for i in range(1, 4):
        c = copy(part, whole.at[here], gather_send_sem.at[i - 1], gather_recv_sem.at[i - 1], group[i - 1])
        c.start()
        gathers.append(c)
    for c in gathers:
        c.wait_recv()
    for p in range(4):
        gq_ref[:, p * 256 : (p + 1) * 256] = whole[p, 0:8, :]
        if p < 2:
            gq_ref[:, 1024 + p * 256 : 1280 + p * 256] = whole[p, 8:16, :]
        else:
            go_ref[:, (p - 2) * 256 : (p - 1) * 256] = whole[p, 8:16, :]
    for c in pair + [relay_up, relay_dn, up_b, dn_a, up_a, dn_b] + lines + columns + gathers:
        c.wait_send()


def body(inputs, cotangent, w_qkv, w_out, gain, logit_scale):
    vmem = pl.BlockSpec(memory_space=pltpu.VMEM)
    scale_cols = jnp.repeat((logit_scale * LOG2E).reshape(2, 8), TOK, axis=1)
    scale_lanes = jnp.repeat(logit_scale.reshape(2, 8), 32, axis=1)
    head = jnp.arange(256) // 32
    ones_blk = (head[:, None] == head[None, :]).astype(BF)
    ones_big = ((jnp.arange(KEYS) // TOK)[:, None] == head[None, :]).astype(BF)
    dma = pltpu.SemaphoreType.DMA
    blocks = pltpu.VMEM((8, TOK, WIDTH), BF)
    pieces = pltpu.VMEM((3, 80, WIDTH), BF)
    out, grad_in, grads = pl.pallas_call(
        attention_kernel,
        out_shape=[
            jax.ShapeDtypeStruct(inputs.shape, BF),
            jax.ShapeDtypeStruct(inputs.shape, BF),
            jax.ShapeDtypeStruct((2, 4, 4, 8, 16, 256), BF),
        ],
        in_specs=[vmem] * 9,
        out_specs=[vmem] * 3,
        scratch_shapes=[blocks] * 6
        + [pieces] * 4
        + [
            pltpu.VMEM((TOK, 3 * WIDTH), BF),
            pltpu.VMEM((8 * TOK, WIDTH), BF),
            pltpu.VMEM((8 * TOK, WIDTH), BF),
            pltpu.VMEM((8 * TOK, WIDTH), BF),
            pltpu.VMEM((8 * TOK, 3 * WIDTH), BF),
        ]
        + [dma((7,))] * 4
        + [dma((3,))] * 4,
        compiler_params=pltpu.CompilerParams(
            collective_id=0, has_side_effects=True, vmem_limit_bytes=56 * 2**20
        ),
    )(inputs, cotangent, w_qkv, w_out, gain.reshape(1, WIDTH), scale_cols, scale_lanes, ones_big, ones_blk)
    share_qkv, share_out = pl.pallas_call(
        reduce_kernel,
        out_shape=[jax.ShapeDtypeStruct((8, 1536), F32), jax.ShapeDtypeStruct((8, 512), F32)],
        in_specs=[vmem],
        out_specs=[vmem] * 2,
        scratch_shapes=[
            pltpu.VMEM((4, 4, 8, 16, 256), BF),
            pltpu.VMEM((4, 4, 8, 16, 256), BF),
            pltpu.VMEM((2, 2, 8, 16, 256), BF),
            pltpu.VMEM((2, 4, 8, 16, 256), BF),
            pltpu.VMEM((4, 8, 16, 256), BF),
            pltpu.VMEM((3, 8, 16, 256), BF),
            pltpu.VMEM((8, 16, 256), BF),
            pltpu.VMEM((7, 16, 256), BF),
            pltpu.VMEM((16, 256), F32),
            pltpu.VMEM((4, 16, 256), F32),
        ]
        + [dma((4,))] * 2
        + [dma((2,))] * 2
        + [dma((4,))] * 2
        + [dma((3,))] * 2
        + [dma((7,))] * 2
        + [dma((3,))] * 2,
        compiler_params=pltpu.CompilerParams(
            collective_id=1, has_side_effects=True, vmem_limit_bytes=32 * 2**20
        ),
    )(grads)
    return out, grad_in, share_qkv, share_out.T


def solution(mesh):
    placed = (P(None, "lat", "lon", None), P(None, "lat", "lon", None), P(), P(), P(), P())
    return jax.shard_map(
        body,
        mesh=mesh,
        in_specs=placed,
        out_specs=(
            P(None, "lat", "lon", None),
            P(None, "lat", "lon", None),
            P("lon", None),
            P(None, "lon"),
        ),
        check_vma=False,
    )
```

time: 1510 us -> 117 us (0.08)
  waiting for transfers between devices: 1210 us -> 0 us
  matrix products: 124 us -> 0 us
  Pallas kernels: 0 us -> 101 us
  local copies, waits for them, and re-layouts: 78.4 us -> 13.3 us
  other arithmetic: 53.2 us -> 2.46 us
  starting transfers between devices: 19.4 us -> 0 us
    reduce_scatter x2 -> x0, waiting for transfers between devices: 1100 us -> none  [the longest x1 835 us: body(): lax.psum_scatter(summed[0], 'lon', scatter_dimension=0, tiled=True)]
    dot_general x96 -> x0, matrix products: 124 us -> none  [the longest x8 20.2 us: window_pass(): jnp.dot((x_win * keep_b).T, dqkv, preferred_element_type=jnp.float32)]
    pallas_call x0 -> x2, Pallas kernels: none -> 101 us  [the longest x1 71.3 us: body(): pl.pallas_call(attention_kernel, out_shape=[jax.ShapeDtypeStruct(inputs.s...]
    psum x1 -> x0, waiting for transfers between devices: 63.1 us -> none  [body(): lax.psum(grad_qkv.astype(jnp.bfloat16), 'lat').astype(jnp.float32)]
    ppermute x8 -> x0, waiting for transfers between devices: 45 us -> none  [from_behind(): return lax.ppermute(value, axis, pairs)]
    while x291 -> x0, local copies, waits for them, and re-layouts: 41 us -> none
    ppermute x8 -> x0, starting transfers between devices: 19.1 us -> none  [from_behind(): return lax.ppermute(value, axis, pairs)]
    convert_element_type x22 -> x2, other arithmetic: 18.7 us -> 1.79 us  [the longest x1 1.03 us: body(): ones_big = ((jnp.arange(KEYS) // TOK)[:, None] == head[None, :]).astype(BF)]
  transfers between devices with their start and end apart: 11 -> 0, of which waited for: 7 -> 0; matrix products, arithmetic and copies ran while one was open for 1% -> 0% of each run, Pallas kernels for 0% -> 0%
where the time goes in v1:
time: 117 us
  Pallas kernels  101 us (86%)
  local copies, waits for them, and re-layouts  13.3 us (11%)
  other arithmetic  2.46 us (2%)
    pallas_call x1, Pallas kernels, body(): pl.pallas_call(attention_kernel, out_shape=[jax.ShapeDtypeStruct(inputs.s...  71.3 us
    pallas_call x1, Pallas kernels, body(): pl.pallas_call(reduce_kernel, out_shape=[jax.ShapeDtypeStruct((8, 1536),...  29.5 us
    unnamed x12, local copies, waits for them, and re-layouts  11 us

profile of v1, /device:TPU:1, one launch (start us, length us, event | category | flops | bytes accessed | tf_op | source)
XLA Modules:
  0.0 117.2 jit_solution(4578326380022798869)
XLA Ops:
  0.6 0.7 broadcast_multiply_fusion
  1.3 0.1 reshape.63
  1.4 0.7 reshape.65
  2.1 0.1 broadcast_in_dim.5
  2.2 0.7 reshape.66.scale_lanes
  2.9 0.1 broadcast_in_dim.4
  2.9 0.7 reshape.64.scale_cols
  3.6 0.8 compare_convert_fusion.1.ones_blk
  4.4 0.0 copy-start.2
  4.4 1.0 compare_convert_fusion.ones_big
  5.4 3.1 %copy.10.x_ref = bf16[2,48,12,512]{3,2,1,0:T(8,128)(2,1)} copy(bf16[2,48,12,512]{3,1,2,0:T(8,128)(2,1)} %param.6) | data formatting | bytes 2359296 | tf_op args[0]
  8.5 0.0 copy-done.2
  8.5 1.8 %copy.11.g_ref = bf16[2,48,12,512]{3,2,1,0:T(8,128)(2,1)} copy(bf16[2,48,12,512]{3,1,2,0:T(8,128)(2,1)S(1)} %copy-done.2) | data formatting | bytes 2359296 | tf_op args[1]
  10.3 71.3 %shard_map.93 = (bf16[2,48,12,512]{3,2,1,0:T(8,128)(2,1)}, bf16[2,48,12,512]{3,2,1,0:T(8,128)(2,1)}, bf16[2,4,4,8,16,256]{5,4,3,2,1,0:T(8,128)(2,1)}) custom-call(bf16[2,48,12,512]{3,2,1,0:T(8,128)(2,1)} %copy.10.x_ref, bf16[2,48,12,512]{3,2,1,0:T(8,128)(2,1)} %copy.11.g_ref, bf16[512,1536]{1,0:T(8,128)(2,1)} %w_qkv.1, bf16[512,512]{1,0:T(8,128)(2,1)} %w_out.1, ...), custom_call_target="tpu_custom_call" | custom-call | tf_op jit(solution)/shard_map/pallas_call | solution.py:551
  81.6 0.0 copy-start
  81.6 3.2 %copy.12 = bf16[2,48,12,512]{3,1,2,0:T(8,128)(2,1)} copy(bf16[2,48,12,512]{3,2,1,0:T(8,128)(2,1)} %get-tuple-element.14) | data formatting | bytes 2359296
  84.8 0.0 copy-done
  84.8 0.0 copy-start.1
  84.8 29.5 %shard_map.94 = (f32[8,1536]{1,0:T(8,128)S(1)}, f32[8,512]{1,0:T(8,128)S(1)}) custom-call(bf16[2,4,4,8,16,256]{5,4,3,2,1,0:T(8,128)(2,1)S(1)} %copy-done), custom_call_target="tpu_custom_call" | custom-call | tf_op jit(solution)/shard_map/pallas_call | solution.py:575
  114.3 0.0 copy-done.1
  114.3 1.7 %copy.13 = bf16[2,48,12,512]{3,1,2,0:T(8,128)(2,1)} copy(bf16[2,48,12,512]{3,2,1,0:T(8,128)(2,1)S(1)} %copy-done.1) | data formatting | bytes 2359296
  116.0 0.6 copy.16
  116.6 0.6 copy.17
  (2 shorter events, 0.0 us)
Async XLA Ops:
  4.4 4.1 %copy-start.2 = (bf16[2,48,12,512]{3,1,2,0:T(8,128)(2,1)S(1)}, bf16[2,48,12,512]{3,1,2,0:T(8,128)(2,1)}, u32[]{:S(2)}) copy-start(bf16[2,48,12,512]{3,1,2,0:T(8,128)(2,1)} %param.7) | copy-start | bytes 3538948
  81.6 3.2 %copy-start = (bf16[2,4,4,8,16,256]{5,4,3,2,1,0:T(8,128)(2,1)S(1)}, bf16[2,4,4,8,16,256]{5,4,3,2,1,0:T(8,128)(2,1)}, u32[]{:S(2)}) copy-start(bf16[2,4,4,8,16,256]{5,4,3,2,1,0:T(8,128)(2,1)} %get-tuple-element.11.grads_ref) | copy-start | bytes 6291460
  84.8 29.5 %copy-start.1 = (bf16[2,48,12,512]{3,2,1,0:T(8,128)(2,1)S(1)}, bf16[2,48,12,512]{3,2,1,0:T(8,128)(2,1)}, u32[]{:S(2)}) copy-start(bf16[2,48,12,512]{3,2,1,0:T(8,128)(2,1)} %get-tuple-element.15) | copy-start | bytes 3538948

commit v2 on v1

v2 whole, which is shorter than its diff:
```python
import jax
import jax.numpy as jnp
from jax import lax
from jax.experimental import pallas as pl
from jax.experimental.pallas import tpu as pltpu
from jax.sharding import PartitionSpec as P

BF = jnp.bfloat16
F32 = jnp.float32
MESH = pl.DeviceIdType.MESH
HEADS = 16
WIDTH = 512
HALF = 72
TOK = 144
QUART = 36
KEYS = 8 * TOK
LOG2E = 1.4426950408889634
FLOOR = 1e-6
EPS = 1e-5


def nn(a, b):
    return jnp.dot(a, b, preferred_element_type=F32)


def nt(a, b):
    return lax.dot_general(a, b, (((1,), (1,)), ((), ())), preferred_element_type=F32)


def tn(a, b):
    return lax.dot_general(a, b, (((0,), (0,)), ((), ())), preferred_element_type=F32)


def spread(part):
    head = lax.broadcasted_iota(jnp.int32, part.shape, 1) // 32
    zero = jnp.zeros_like(part)
    return jnp.concatenate([jnp.where(head == h, part, zero) for h in range(8)], axis=0)


def pick(full):
    head = lax.broadcasted_iota(jnp.int32, (TOK, 256), 1) // 32
    chosen = full[:TOK]
    for h in range(1, 8):
        chosen = jnp.where(head == h, full[h * TOK : (h + 1) * TOK], chosen)
    return chosen


def head_sum(value, ones_block):
    return nn(value.astype(BF), ones_block)


def head_sum_fine(value, ones_block):
    high = value.astype(BF)
    low = (value - high.astype(F32)).astype(BF)
    return nn(high, ones_block) + nn(low, ones_block)


def pair_math(x, gw, split, w_qkv, w_qkv_t, w_out, w_out_t, gain, scale_cols, scale_lanes, ones_big, ones_big_t, ones_blk):
    ones_block = ones_blk[...]
    qkv = nn(x, w_qkv[...]).astype(BF)
    row = lax.broadcasted_iota(jnp.int32, (TOK, 1), 0)
    col = lax.broadcasted_iota(jnp.int32, (1, KEYS), 1)
    allowed = jnp.where(split, (row // QUART) % 2, 0) == jnp.where(split, (col // QUART) % 2, 0)
    vec = []
    for half in range(2):
        lo = half * 256
        q = qkv[:, lo : lo + 256].astype(F32)
        k = qkv[:, 512 + lo : 768 + lo].astype(F32)
        q_len = jnp.sqrt(head_sum_fine(q * q, ones_block))
        k_len = jnp.sqrt(head_sum_fine(k * k, ones_block))
        q_inv = 1.0 / jnp.maximum(q_len, FLOOR)
        k_inv = 1.0 / jnp.maximum(k_len, FLOOR)
        uq = q * q_inv
        uk = k * k_inv
        vec.append((q_len, k_len, q_inv, k_inv, uq, uk, uq.astype(BF), uk.astype(BF)))
    att = [[None, None], [None, None]]
    saved = {}
    for g in range(2):
        r = slice(g * TOK, (g + 1) * TOK)
        for half in range(2):
            lo = half * 256
            uq, uk = vec[half][6][r], vec[half][7][r]
            k_big = spread(uk)
            v_big = spread(qkv[r, 1024 + lo : 1280 + lo])
            e = jnp.exp2(nt(uq, k_big) * scale_cols[half : half + 1, :])
            if g == 1:
                e = jnp.where(allowed, e, 0.0)
            e = e.astype(BF)
            both = nn(e, jnp.concatenate([v_big, ones_big[...]], axis=1))
            r_den = 1.0 / both[:, 256:]
            att[g][half] = (both[:, :256] * r_den).astype(BF)
            saved[g, half] = (k_big, v_big, e, r_den, uq)
    att_b = jnp.concatenate([jnp.concatenate(one, axis=1) for one in att], axis=0)
    proj = nn(att_b, w_out[...])
    dev = proj - jnp.mean(proj, -1, keepdims=True)
    inv = lax.rsqrt(jnp.mean(dev * dev, -1, keepdims=True) + EPS)
    normed = dev * inv
    branch = gain * normed
    up = gain * gw
    dproj = (
        (up - jnp.mean(up, -1, keepdims=True) - normed * jnp.mean(up * normed, -1, keepdims=True))
        * inv
    ).astype(BF)
    datt = nn(dproj, w_out_t[...]).astype(BF)
    dq, dk, dv = {}, {}, {}
    for g in range(2):
        r = slice(g * TOK, (g + 1) * TOK)
        for half in range(2):
            lo = half * 256
            k_big, v_big, e, r_den, uq = saved[g, half]
            dh = datt[r, lo : lo + 256].astype(F32) * r_den
            dh_b = dh.astype(BF)
            dd = (dh * att[g][half].astype(F32)).astype(BF)
            t = nt(dh_b, v_big) - nn(dd, ones_big_t[...])
            ds = (e.astype(F32) * t).astype(BF)
            lanes = scale_lanes[half : half + 1, :]
            dq[g, half] = nn(ds, k_big) * lanes
            dk[g, half] = pick(tn(ds, uq)) * lanes
            dv[g, half] = pick(tn(e, dh_b)).astype(BF)
    cols = [None] * 6
    for half in range(2):
        q_len, k_len, q_inv, k_inv, uq, uk, _, _ = vec[half]
        duq = jnp.concatenate([dq[0, half], dq[1, half]], axis=0)
        duk = jnp.concatenate([dk[0, half], dk[1, half]], axis=0)
        q_tail = jnp.where(q_len > FLOOR, uq * head_sum(uq * duq, ones_block), 0.0)
        k_tail = jnp.where(k_len > FLOOR, uk * head_sum(uk * duk, ones_block), 0.0)
        cols[half] = ((duq - q_tail) * q_inv).astype(BF)
        cols[2 + half] = ((duk - k_tail) * k_inv).astype(BF)
        cols[4 + half] = jnp.concatenate([dv[0, half], dv[1, half]], axis=0)
    dqkv = jnp.concatenate(cols, axis=1)
    dshifted = nn(dqkv, w_qkv_t[...])
    return branch, dshifted, att_b, dproj, dqkv


def pack(ref, first_row, rows, first_col):
    low = first_row // 16 * 16
    high = (first_row + rows + 15) // 16 * 16
    parts = []
    for lev in range(2):
        for c in range(first_col, first_col + 6):
            strip = ref[lev, c, low:high, :].astype(F32)
            parts.append(strip[first_row - low : first_row - low + rows])
    return jnp.concatenate(parts, axis=0)


def piece_of(x_part, g_part):
    pad = jnp.zeros((4, WIDTH), F32)
    return jnp.concatenate([x_part, pad, g_part, pad], axis=0).astype(BF)


def unpiece(ref):
    whole = ref.astype(F32)
    return whole[:QUART], whole[40 : 40 + QUART]


def block_kernel(
    x_ref,
    g_ref,
    w_qkv,
    w_out,
    gain_ref,
    scale_ref,
    out_ref,
    gin_ref,
    gq_ref,
    go_ref,
    send,
    recv,
    own,
    back_send,
    back_recv,
    own_res,
    send7,
    recv7,
    back7_send,
    back7_recv,
    x_all,
    att_all,
    dproj_all,
    dqkv_all,
    w_qkv_t,
    w_out_t,
    ones_big,
    ones_big_t,
    ones_blk,
    scale_cols,
    scale_lanes,
    grads,
    pair_recv,
    mine,
    ring_relay,
    ring_recv,
    cut,
    line_recv,
    piece,
    z_recv,
    part,
    whole,
    send_sem,
    recv_sem,
    back_send_sem,
    back_recv_sem,
    send7_sem,
    recv7_sem,
    back7_send_sem,
    back7_recv_sem,
    pair_send_sem,
    pair_recv_sem,
    relay_send_sem,
    relay_recv_sem,
    ring_send_sem,
    ring_recv_sem,
    line_send_sem,
    line_recv_sem,
    z_send_sem,
    z_recv_sem,
    gather_send_sem,
    gather_recv_sem,
):
    n_lat = lax.axis_size("lat")
    n_lon = lax.axis_size("lon")
    a = lax.axis_index("lat")
    b = lax.axis_index("lon")

    def mod(value, n):
        return lax.rem(value + n, n)

    up_a, dn_a = mod(a + 1, n_lat), mod(a - 1, n_lat)
    up_b, dn_b = mod(b + 1, n_lon), mod(b - 1, n_lon)
    core, y_lo = lax.rem(a, 2), a // 2
    z, y_hi, x = b // 8, lax.rem(b // 4, 2), lax.rem(b, 4)
    y = 2 * y_hi + y_lo
    u = x * (1 - core) + y * core
    v = y * (1 - core) + x * core

    def device(uu, vv, zz):
        xx = uu * (1 - core) + vv * core
        yy = vv * (1 - core) + uu * core
        return (2 * lax.rem(yy, 2) + core, zz * 8 + (yy // 2) * 4 + xx)

    partner = (a + 1 - 2 * core, b)
    nxt = device(mod(u + 1, 4), v, z)
    prv = device(mod(u + 3, 4), v, z)
    line = [device(u, mod(v + i, 4), z) for i in range(1, 4)]
    column = [device(u, v, mod(z + i, 8)) for i in range(1, 8)]
    group = [(mod(a + i, 4), b) for i in range(1, 4)]
    around = [(a, up_b), (a, dn_b), (up_a, b), (dn_a, b), (up_a, dn_b), (dn_a, up_b)]
    peers = around + [partner, nxt, prv] + line + column + group

    barrier = pltpu.get_barrier_semaphore()
    for peer in peers:
        pl.semaphore_signal(barrier, inc=1, device_id=peer, device_id_type=MESH)

    def copy(src, dst, send_sem, recv_sem, peer):
        return pltpu.make_async_remote_copy(
            src_ref=src, dst_ref=dst, send_sem=send_sem, recv_sem=recv_sem, device_id=peer, device_id_type=MESH
        )

    def forth(w, peer):
        return copy(send.at[w], recv.at[w], send_sem.at[w], recv_sem.at[w], peer)

    def back(w, peer):
        return copy(back_send.at[w], back_recv.at[w], back_send_sem.at[w], back_recv_sem.at[w], peer)

    def forth7(j):
        peer = ((a, up_b), (dn_a, b), (dn_a, up_b))[j]
        return copy(send7.at[j], recv7.at[j], send7_sem.at[j], recv7_sem.at[j], peer)

    def back7(j):
        peer = ((a, dn_b), (up_a, b), (up_a, dn_b))[j]
        return copy(back7_send.at[j], back7_recv.at[j], back7_send_sem.at[j], back7_recv_sem.at[j], peer)

    def both(w, first_col):
        return jnp.concatenate(
            [pack(x_ref, 6 * w + 3, 6, first_col), pack(g_ref, 6 * w + 3, 6, first_col)], axis=0
        ).astype(BF)

    for w in range(7):
        send[w] = both(w, 6 * (w % 2))
        if w == 0:
            pl.semaphore_wait(barrier, len(peers))
        forth(w, (a, up_b) if w % 2 else (a, dn_b)).start()
    for j, (first_row, first_col) in enumerate(((45, 6), (0, 0), (0, 6))):
        send7[j] = piece_of(pack(x_ref, first_row, 3, first_col), pack(g_ref, first_row, 3, first_col))
        forth7(j).start()

    for w in range(7):
        own[w] = both(w, 6 - 6 * (w % 2))

    w_qkv_t[...] = w_qkv[...].T
    w_out_t[...] = w_out[...].T
    head = lax.broadcasted_iota(jnp.int32, (KEYS, 256), 1) // 32
    ones_big[...] = jnp.where(lax.broadcasted_iota(jnp.int32, (KEYS, 256), 0) // TOK == head, 1.0, 0.0).astype(BF)
    head = lax.broadcasted_iota(jnp.int32, (256, KEYS), 0) // 32
    ones_big_t[...] = jnp.where(lax.broadcasted_iota(jnp.int32, (256, KEYS), 1) // TOK == head, 1.0, 0.0).astype(BF)
    head = lax.broadcasted_iota(jnp.int32, (256, 256), 1) // 32
    ones_blk[...] = jnp.where(lax.broadcasted_iota(jnp.int32, (256, 256), 0) // 32 == head, 1.0, 0.0).astype(BF)
    for half in range(2):
        key_head = lax.broadcasted_iota(jnp.int32, (1, KEYS), 1) // TOK
        lane_head = lax.broadcasted_iota(jnp.int32, (1, 256), 1) // 32
        keys = jnp.zeros((1, KEYS), F32)
        lanes = jnp.zeros((1, 256), F32)
        for h in range(8):
            keys = jnp.where(key_head == h, scale_ref[half * 8 + h] * LOG2E, keys)
            lanes = jnp.where(lane_head == h, scale_ref[half * 8 + h], lanes)
        scale_cols[half : half + 1, :] = keys
        scale_lanes[half : half + 1, :] = lanes

    @pl.loop(0, 4)
    def _(pair):
        w = 2 * pair
        forth(w, (a, up_b)).wait_recv()

        @pl.when(pair < 3)
        def _():
            forth(w + 1, (a, up_b)).wait_recv()

        @pl.when(pair == 3)
        def _():
            for j in range(3):
                forth7(j).wait_recv()
            low_x, low_g = pack(x_ref, 45, 3, 0), pack(g_ref, 45, 3, 0)
            side_x, side_g = unpiece(recv7[0])
            down_x, down_g = unpiece(recv7[1])
            diag_x, diag_g = unpiece(recv7[2])
            own[7] = jnp.concatenate([low_x, down_x, low_g, down_g], axis=0).astype(BF)
            recv[7] = jnp.concatenate([side_x, diag_x, side_g, diag_g], axis=0).astype(BF)

        blocks = [ref[w + i].astype(F32) for i in range(2) for ref in (own, recv)]
        xw = jnp.concatenate([block[:HALF] for block in blocks], axis=0).astype(BF)
        gw = jnp.concatenate([block[HALF:] for block in blocks], axis=0)
        split = jnp.logical_and(pair == 3, a == n_lat - 1)
        branch, dshifted, att, dproj, dqkv = pair_math(
            xw,
            gw,
            split,
            w_qkv,
            w_qkv_t,
            w_out,
            w_out_t,
            gain_ref[...],
            scale_cols,
            scale_lanes,
            ones_big,
            ones_big_t,
            ones_blk,
        )
        for i in range(2):
            at = i * TOK
            own_res[w + i] = jnp.concatenate(
                [branch[at : at + HALF], dshifted[at : at + HALF]], axis=0
            ).astype(BF)
            back_send[w + i] = jnp.concatenate(
                [branch[at + HALF : at + TOK], dshifted[at + HALF : at + TOK]], axis=0
            ).astype(BF)
        back(w, (a, up_b)).start()

        @pl.when(pair < 3)
        def _():
            back(w + 1, (a, dn_b)).start()

        rows = pl.ds(pl.multiple_of(pair * 2 * TOK, 2 * TOK), 2 * TOK)
        x_all[rows, :] = xw
        att_all[rows, :] = att
        dproj_all[rows, :] = dproj
        dqkv_all[rows, :] = dqkv

    ours = own_res[7].astype(F32)
    theirs = back_send[7].astype(F32)
    back7_send[0] = piece_of(theirs[:QUART], theirs[HALF : HALF + QUART])
    back7_send[1] = piece_of(ours[QUART:HALF], ours[HALF + QUART :])
    back7_send[2] = piece_of(theirs[QUART:HALF], theirs[HALF + QUART :])
    for j in range(3):
        back7(j).start()

    @pl.loop(0, 2)
    def _(side):
        owner = core * side + (1 - core) * (1 - side)
        at = pl.multiple_of(owner * 768, 256)
        chunks = [tn(x_all[...], dqkv_all[:, pl.ds(at + i * 256, 256)]) for i in range(3)]
        chunks.append(tn(dproj_all[...], att_all[:, pl.ds(pl.multiple_of(owner * 256, 256), 256)]))
        for low in range(2):
            halves = [chunk.reshape(64, 8, 256) for chunk in chunks[2 * low : 2 * low + 2]]
            joined = jnp.concatenate(halves, axis=1).astype(BF)
            for lon in range(64):
                zz, yy, xx = lon // 8, 2 * ((lon // 4) % 2) + low, lon % 4
                uu = xx * (1 - owner) + yy * owner
                vv = yy * (1 - owner) + xx * owner
                grads[side, uu, vv, zz] = joined[lon]

    order = (2, 1, 3, 0)
    pairs = []
    for i, step in enumerate(order):
        c = copy(grads.at[0, mod(v + step, 4)], pair_recv.at[i], pair_send_sem.at[i], pair_recv_sem.at[i], partner)
        c.start()
        pairs.append(c)

    def add_pair(i):
        pairs[i].wait_recv()
        chunk = mod(u + order[i], 4)

        @pl.loop(0, 4)
        def _(vv):
            mine[i, vv] = (grads[1, chunk, vv].astype(F32) + pair_recv[i, vv].astype(F32)).astype(BF)

    def halves_of(w, left):
        came = (w % 2 == 0) == left
        block = (back_recv if came else own_res)[w].astype(F32)
        return block[:HALF], block[HALF:]

    def assemble(lev, left, tops, lows):
        parts = [halves_of(w, left) for w in range(7)]
        for c in range(6):
            at = lev * 6 + c
            for k, (ref, dst) in enumerate(((x_ref, out_ref), (g_ref, gin_ref))):
                strip = (
                    [tops[k][at * 3 : at * 3 + 3]]
                    + [one[k][at * 6 : at * 6 + 6] for one in parts]
                    + [lows[k][at * 3 : at * 3 + 3]]
                )
                cc = c if left else c + 6
                dst[lev, cc] = (ref[lev, cc].astype(F32) + jnp.concatenate(strip, axis=0)).astype(BF)

    add_pair(0)
    relay_up = copy(mine.at[0, pl.ds(0, 2)], ring_relay.at[0], relay_send_sem.at[0], relay_recv_sem.at[0], nxt)
    relay_dn = copy(mine.at[0, pl.ds(2, 2)], ring_relay.at[1], relay_send_sem.at[1], relay_recv_sem.at[1], prv)
    relay_up.start()
    relay_dn.start()
    add_pair(1)
    ring_up_b = copy(mine.at[1, pl.ds(2, 2)], ring_recv.at[0, pl.ds(2, 2)], ring_send_sem.at[0], ring_recv_sem.at[0], nxt)
    ring_up_b.start()
    add_pair(2)
    ring_dn_a = copy(mine.at[2, pl.ds(0, 2)], ring_recv.at[1, pl.ds(0, 2)], ring_send_sem.at[1], ring_recv_sem.at[1], prv)
    ring_dn_a.start()
    add_pair(3)
    relay_up.wait_recv()

    @pl.loop(0, 2)
    def _(vv):
        mine[1, vv] = (mine[1, vv].astype(F32) + ring_relay[0, vv].astype(F32)).astype(BF)

    ring_up_a = copy(mine.at[1, pl.ds(0, 2)], ring_recv.at[0, pl.ds(0, 2)], ring_send_sem.at[2], ring_recv_sem.at[2], nxt)
    ring_up_a.start()
    relay_dn.wait_recv()

    @pl.loop(0, 2)
    def _(vv):
        mine[2, 2 + vv] = (mine[2, 2 + vv].astype(F32) + ring_relay[1, vv].astype(F32)).astype(BF)

    ring_dn_b = copy(mine.at[2, pl.ds(2, 2)], ring_recv.at[1, pl.ds(2, 2)], ring_send_sem.at[3], ring_recv_sem.at[3], prv)
    ring_dn_b.start()

    for w in range(7):
        back(w, (a, up_b)).wait_recv()
    for j in range(3):
        back7(j).wait_recv()
    block = own_res[7].astype(F32)
    near = (block[:QUART], block[HALF : HALF + QUART])
    side, down, diag = (unpiece(back7_recv[j]) for j in range(3))
    assemble(0, True, down, near)
    assemble(0, False, diag, side)

    for c in (ring_up_b, ring_dn_a, ring_up_a, ring_dn_b):
        c.wait_recv()

    @pl.loop(0, 4)
    def _(vv):
        cut[vv] = (
            mine[3, vv].astype(F32) + ring_recv[0, vv].astype(F32) + ring_recv[1, vv].astype(F32)
        ).astype(BF)

    lines = []
    for i in range(3):
        c = copy(cut.at[mod(v + i + 1, 4)], line_recv.at[i], line_send_sem.at[i], line_recv_sem.at[i], line[i])
        c.start()
        lines.append(c)
    assemble(1, True, down, near)
    for c in lines:
        c.wait_recv()
    piece[...] = (
        cut[v].astype(F32) + line_recv[0].astype(F32) + line_recv[1].astype(F32) + line_recv[2].astype(F32)
    ).astype(BF)
    columns = []
    for i in range(7):
        c = copy(piece.at[mod(z + i + 1, 8)], z_recv.at[i], z_send_sem.at[i], z_recv_sem.at[i], column[i])
        c.start()
        columns.append(c)
    assemble(1, False, diag, side)
    for c in columns:
        c.wait_recv()
    total = piece[z].astype(F32)
    for i in range(7):
        total = total + z_recv[i].astype(F32)
    part[...] = total

    here = 2 * core + y_lo
    whole[here] = total
    gathers = []
    for i in range(3):
        c = copy(part, whole.at[here], gather_send_sem.at[i], gather_recv_sem.at[i], group[i])
        c.start()
        gathers.append(c)

    for w in range(7):
        forth(w, (a, up_b)).wait_send()
        back(w, (a, up_b)).wait_send()
    for j in range(3):
        forth7(j).wait_send()
        back7(j).wait_send()
    for c in pairs + [relay_up, relay_dn, ring_up_b, ring_dn_a, ring_up_a, ring_dn_b] + lines + columns:
        c.wait_send()
    for c in gathers:
        c.wait_recv()
    for owner in range(2):
        at = owner * 768
        gq_ref[:, at : at + 256] = whole[2 * owner, 0:8, :]
        gq_ref[:, at + 256 : at + 512] = whole[2 * owner, 8:16, :]
        gq_ref[:, at + 512 : at + 768] = whole[2 * owner + 1, 0:8, :]
        go_ref[:, owner * 256 : owner * 256 + 256] = whole[2 * owner + 1, 8:16, :]
    for c in gathers:
        c.wait_send()


def body(inputs, cotangent, w_qkv, w_out, gain, logit_scale):
    vmem = pl.BlockSpec(memory_space=pltpu.VMEM)
    smem = pl.BlockSpec(memory_space=pltpu.SMEM)
    dma = pltpu.SemaphoreType.DMA
    blocks = pltpu.VMEM((8, TOK, WIDTH), BF)
    pieces = pltpu.VMEM((3, 80, WIDTH), BF)
    x_view = inputs.transpose(0, 2, 1, 3)
    g_view = cotangent.transpose(0, 2, 1, 3)
    out, grad_in, share_qkv, share_out = pl.pallas_call(
        block_kernel,
        out_shape=[
            jax.ShapeDtypeStruct(x_view.shape, BF),
            jax.ShapeDtypeStruct(x_view.shape, BF),
            jax.ShapeDtypeStruct((8, 3 * WIDTH), F32),
            jax.ShapeDtypeStruct((8, WIDTH), F32),
        ],
        in_specs=[vmem] * 5 + [smem],
        out_specs=[vmem] * 4,
        scratch_shapes=[blocks] * 6
        + [pieces] * 4
        + [
            pltpu.VMEM((8 * TOK, WIDTH), BF),
            pltpu.VMEM((8 * TOK, WIDTH), BF),
            pltpu.VMEM((8 * TOK, WIDTH), BF),
            pltpu.VMEM((8 * TOK, 3 * WIDTH), BF),
            pltpu.VMEM((3 * WIDTH, WIDTH), BF),
            pltpu.VMEM((WIDTH, WIDTH), BF),
            pltpu.VMEM((KEYS, 256), BF),
            pltpu.VMEM((256, KEYS), BF),
            pltpu.VMEM((256, 256), BF),
            pltpu.VMEM((2, KEYS), F32),
            pltpu.VMEM((2, 256), F32),
            pltpu.VMEM((2, 4, 4, 8, 16, 256), BF),
            pltpu.VMEM((4, 4, 8, 16, 256), BF),
            pltpu.VMEM((4, 4, 8, 16, 256), BF),
            pltpu.VMEM((2, 2, 8, 16, 256), BF),
            pltpu.VMEM((2, 4, 8, 16, 256), BF),
            pltpu.VMEM((4, 8, 16, 256), BF),
            pltpu.VMEM((3, 8, 16, 256), BF),
            pltpu.VMEM((8, 16, 256), BF),
            pltpu.VMEM((7, 16, 256), BF),
            pltpu.VMEM((16, 256), F32),
            pltpu.VMEM((4, 16, 256), F32),
        ]
        + [dma((7,))] * 4
        + [dma((3,))] * 4
        + [dma((4,))] * 2
        + [dma((2,))] * 2
        + [dma((4,))] * 2
        + [dma((3,))] * 2
        + [dma((7,))] * 2
        + [dma((3,))] * 2,
        compiler_params=pltpu.CompilerParams(
            collective_id=0, has_side_effects=True, vmem_limit_bytes=56 * 2**20
        ),
    )(x_view, g_view, w_qkv, w_out, gain.reshape(1, WIDTH), logit_scale)
    return out.transpose(0, 2, 1, 3), grad_in.transpose(0, 2, 1, 3), share_qkv, share_out.T


def solution(mesh):
    placed = (P(None, "lat", "lon", None), P(None, "lat", "lon", None), P(), P(), P(), P())
    return jax.shard_map(
        body,
        mesh=mesh,
        in_specs=placed,
        out_specs=(
            P(None, "lat", "lon", None),
            P(None, "lat", "lon", None),
            P("lon", None),
            P(None, "lon"),
        ),
        check_vma=False,
    )
```

time: 117 us -> 82.6 us (0.71)
  Pallas kernels: 101 us -> 77.2 us
  local copies, waits for them, and re-layouts: 13.3 us -> 4.71 us
  other arithmetic: 2.46 us -> 0 us
    pallas_call x2 -> x1, Pallas kernels: 101 us -> 77.2 us  [body(): pl.pallas_call(block_kernel, out_shape=[jax.ShapeDtypeStruct(x_view.shape...]
    unnamed x12 -> x10, local copies, waits for them, and re-layouts: 11 us -> 4.71 us
    reshape x4 -> x0, local copies, waits for them, and re-layouts: 2.17 us -> none  [the longest x2 1.39 us: body(): scale_lanes = jnp.repeat(logit_scale.reshape(2, 8), 32, axis=1)]
    convert_element_type x2 -> x0, other arithmetic: 1.79 us -> none  [the longest x1 1.03 us: body(): ones_big = ((jnp.arange(KEYS) // TOK)[:, None] == head[None, :]).astype(BF)]
where the time goes in v2:
time: 82.6 us; the launch traced here: 82.5 us
  Pallas kernels  77.2 us (93%)
  local copies, waits for them, and re-layouts  4.71 us (6%)
    pallas_call x1, Pallas kernels, body(): pl.pallas_call(block_kernel, out_shape=[jax.ShapeDtypeStruct(x_view.shape...  77.2 us
    unnamed x10, local copies, waits for them, and re-layouts  4.71 us

profile of v2, /device:TPU:1, one launch (start us, length us, event | category | flops | bytes accessed | tf_op | source)
XLA Modules:
  0.0 82.5 jit_solution(15087191965653701690)
XLA Ops:
  0.6 77.2 %shard_map.93 = (bf16[2,12,48,512]{3,2,1,0:T(8,128)(2,1)}, bf16[2,12,48,512]{3,2,1,0:T(8,128)(2,1)}, f32[8,1536]{1,0:T(8,128)}, f32[8,512]{1,0:T(8,128)}) custom-call(bf16[2,12,48,512]{3,2,1,0:T(8,128)(2,1)} %bitcast.8, bf16[2,12,48,512]{3,2,1,0:T(8,128)(2,1)} %bitcast.9, bf16[512,1536]{1,0:T(8,128)(2,1)} %w_qkv.1, bf16[512,512]{1,0:T(8,128)(2,1)} %w_out.1, ...), custom_call_target="tpu_custom_call" | custom-call | tf_op jit(solution)/shard_map/pallas_call | solution.py:532
  77.8 0.0 copy-start
  77.8 2.5 %copy.14 = bf16[2,48,12,512]{3,1,2,0:T(8,128)(2,1)} copy(bf16[2,48,12,512]{3,1,2,0:T(8,128)(2,1)} %bitcast.7) | data formatting | bytes 2359296
  80.3 0.0 copy-done
  80.3 0.0 copy-start.1
  80.3 0.0 copy-start.2
  80.3 1.0 %copy.15 = bf16[2,48,12,512]{3,1,2,0:T(8,128)(2,1)} copy(bf16[2,48,12,512]{3,1,2,0:T(8,128)(2,1)S(1)} %bitcast.6) | data formatting | bytes 2359296
  81.3 0.0 copy-done.1
  81.3 0.6 copy.16
  81.9 0.0 copy-done.2
  81.9 0.6 copy.17
Async XLA Ops:
  77.8 2.5 %copy-start = (bf16[2,12,48,512]{3,2,1,0:T(8,128)(2,1)S(1)}, bf16[2,12,48,512]{3,2,1,0:T(8,128)(2,1)}, u32[]{:S(2)}) copy-start(bf16[2,12,48,512]{3,2,1,0:T(8,128)(2,1)} %get-tuple-element.9) | copy-start | bytes 3538948
  80.3 1.0 %copy-start.1 = (f32[8,1536]{1,0:T(8,128)S(1)}, f32[8,1536]{1,0:T(8,128)}, u32[]{:S(2)}) copy-start(f32[8,1536]{1,0:T(8,128)} %get-tuple-element.18) | copy-start | bytes 147460
  80.3 1.6 %copy-start.2 = (f32[8,512]{1,0:T(8,128)S(1)}, f32[8,512]{1,0:T(8,128)}, u32[]{:S(2)}) copy-start(f32[8,512]{1,0:T(8,128)} %get-tuple-element.11) | copy-start | bytes 49156

commit v3 on v2

--- a/solution.py
+++ b/solution.py
@@ -31,18 +31,40 @@
     return lax.dot_general(a, b, (((0,), (0,)), ((), ())), preferred_element_type=F32)
 
 
+def key_head(place):
+    return jnp.where(place < 1024, place // 128, (place - 1024) // 16)
+
+
+def key_token(place):
+    return jnp.where(place < 1024, place % 128, 128 + (place - 1024) % 16)
+
+
 def spread(part):
     head = lax.broadcasted_iota(jnp.int32, part.shape, 1) // 32
     zero = jnp.zeros_like(part)
-    return jnp.concatenate([jnp.where(head == h, part, zero) for h in range(8)], axis=0)
+    alone = [jnp.where(head == h, part, zero) for h in range(8)]
+    return jnp.concatenate([one[:128] for one in alone] + [one[128:] for one in alone], axis=0)
+
+
+def spread_t(part):
+    main = part[:128].T
+    row = lax.broadcasted_iota(jnp.int32, main.shape, 0) // 32
+    zero = jnp.zeros_like(main)
+    rest = part[128:]
+    head = lax.broadcasted_iota(jnp.int32, rest.shape, 1) // 32
+    last = jnp.concatenate([jnp.where(head == h, rest, jnp.zeros_like(rest)) for h in range(8)], axis=0).T
+    return jnp.concatenate([jnp.where(row == h, main, zero) for h in range(8)] + [last], axis=1)
 
 
 def pick(full):
-    head = lax.broadcasted_iota(jnp.int32, (TOK, 256), 1) // 32
-    chosen = full[:TOK]
-    for h in range(1, 8):
-        chosen = jnp.where(head == h, full[h * TOK : (h + 1) * TOK], chosen)
-    return chosen
+    def choose(first, step, rows):
+        head = lax.broadcasted_iota(jnp.int32, (rows, 256), 1) // 32
+        chosen = full[first : first + rows]
+        for h in range(1, 8):
+            chosen = jnp.where(head == h, full[first + step * h : first + step * h + rows], chosen)
+        return chosen
+
+    return jnp.concatenate([choose(0, 128, 128), choose(1024, 16, 16)], axis=0)
 
 
 def head_sum(value, ones_block):
@@ -55,11 +77,11 @@
     return nn(high, ones_block) + nn(low, ones_block)
 
 
-def pair_math(x, gw, split, w_qkv, w_qkv_t, w_out, w_out_t, gain, scale_cols, scale_lanes, ones_big, ones_big_t, ones_blk):
+def pair_math(x, wait_gw, split, w_qkv, w_out, w_out_t, gain, scale_cols, scale_lanes, ones_big, minus_ones_t, ones_blk):
     ones_block = ones_blk[...]
     qkv = nn(x, w_qkv[...]).astype(BF)
     row = lax.broadcasted_iota(jnp.int32, (TOK, 1), 0)
-    col = lax.broadcasted_iota(jnp.int32, (1, KEYS), 1)
+    col = key_token(lax.broadcasted_iota(jnp.int32, (1, KEYS), 1))
     allowed = jnp.where(split, (row // QUART) % 2, 0) == jnp.where(split, (col // QUART) % 2, 0)
     vec = []
     for half in range(2):
@@ -81,22 +103,23 @@
             lo = half * 256
             uq, uk = vec[half][6][r], vec[half][7][r]
             k_big = spread(uk)
-            v_big = spread(qkv[r, 1024 + lo : 1280 + lo])
-            e = jnp.exp2(nt(uq, k_big) * scale_cols[half : half + 1, :])
+            v = qkv[r, 1024 + lo : 1280 + lo]
+            v_big = spread(v)
+            e = jnp.exp2(nn(uq, spread_t(uk)) * scale_cols[half : half + 1, :])
             if g == 1:
                 e = jnp.where(allowed, e, 0.0)
             e = e.astype(BF)
             both = nn(e, jnp.concatenate([v_big, ones_big[...]], axis=1))
             r_den = 1.0 / both[:, 256:]
             att[g][half] = (both[:, :256] * r_den).astype(BF)
-            saved[g, half] = (k_big, v_big, e, r_den, uq)
+            saved[g, half] = (k_big, v, e, r_den, uq)
     att_b = jnp.concatenate([jnp.concatenate(one, axis=1) for one in att], axis=0)
     proj = nn(att_b, w_out[...])
     dev = proj - jnp.mean(proj, -1, keepdims=True)
     inv = lax.rsqrt(jnp.mean(dev * dev, -1, keepdims=True) + EPS)
     normed = dev * inv
     branch = gain * normed
-    up = gain * gw
+    up = gain * wait_gw()
     dproj = (
         (up - jnp.mean(up, -1, keepdims=True) - normed * jnp.mean(up * normed, -1, keepdims=True))
         * inv
@@ -107,11 +130,14 @@
         r = slice(g * TOK, (g + 1) * TOK)
         for half in range(2):
             lo = half * 256
-            k_big, v_big, e, r_den, uq = saved[g, half]
+            k_big, v, e, r_den, uq = saved[g, half]
             dh = datt[r, lo : lo + 256].astype(F32) * r_den
             dh_b = dh.astype(BF)
             dd = (dh * att[g][half].astype(F32)).astype(BF)
-            t = nt(dh_b, v_big) - nn(dd, ones_big_t[...])
+            t = nn(
+                jnp.concatenate([dh_b, dd], axis=1),
+                jnp.concatenate([spread_t(v), minus_ones_t[...]], axis=0),
+            )
             ds = (e.astype(F32) * t).astype(BF)
             lanes = scale_lanes[half : half + 1, :]
             dq[g, half] = nn(ds, k_big) * lanes
@@ -128,8 +154,7 @@
         cols[2 + half] = ((duk - k_tail) * k_inv).astype(BF)
         cols[4 + half] = jnp.concatenate([dv[0, half], dv[1, half]], axis=0)
     dqkv = jnp.concatenate(cols, axis=1)
-    dshifted = nn(dqkv, w_qkv_t[...])
-    return branch, dshifted, att_b, dproj, dqkv
+    return branch, att_b, dproj, dqkv
 
 
 def pack(ref, first_row, rows, first_col):
@@ -143,6 +168,10 @@
     return jnp.concatenate(parts, axis=0)
 
 
+def padded(part):
+    return jnp.concatenate([part, jnp.zeros((8, WIDTH), F32)], axis=0).astype(BF)
+
+
 def piece_of(x_part, g_part):
     pad = jnp.zeros((4, WIDTH), F32)
     return jnp.concatenate([x_part, pad, g_part, pad], axis=0).astype(BF)
@@ -154,16 +183,22 @@
 
 
 def block_kernel(
+    x_hbm,
+    g_hbm,
+    w_qkv_hbm,
+    w_out_hbm,
+    gain_ref,
+    scale_ref,
+    out_hbm,
+    gin_hbm,
+    gq_ref,
+    go_ref,
     x_ref,
     g_ref,
     w_qkv,
     w_out,
-    gain_ref,
-    scale_ref,
     out_ref,
     gin_ref,
-    gq_ref,
-    go_ref,
     send,
     recv,
     own,
@@ -181,7 +216,7 @@
     w_qkv_t,
     w_out_t,
     ones_big,
-    ones_big_t,
+    minus_ones_t,
     ones_blk,
     scale_cols,
     scale_lanes,
@@ -216,7 +251,15 @@
     z_recv_sem,
     gather_send_sem,
     gather_recv_sem,
+    load_sem,
+    store_sem,
 ):
+    loads = [
+        pltpu.make_async_copy(src, dst, load_sem.at[i])
+        for i, (src, dst) in enumerate(((x_hbm, x_ref), (g_hbm, g_ref), (w_qkv_hbm, w_qkv), (w_out_hbm, w_out)))
+    ]
+    for c in loads:
+        c.start()
     n_lat = lax.axis_size("lat")
     n_lon = lax.axis_size("lon")
     a = lax.axis_index("lat")
@@ -256,8 +299,8 @@
             src_ref=src, dst_ref=dst, send_sem=send_sem, recv_sem=recv_sem, device_id=peer, device_id_type=MESH
         )
 
-    def forth(w, peer):
-        return copy(send.at[w], recv.at[w], send_sem.at[w], recv_sem.at[w], peer)
+    def forth(w, k, peer):
+        return copy(send.at[w, k], recv.at[w, k], send_sem.at[w, k], recv_sem.at[w, k], peer)
 
     def back(w, peer):
         return copy(back_send.at[w], back_recv.at[w], back_send_sem.at[w], back_recv_sem.at[w], peer)
@@ -270,112 +313,129 @@
         peer = ((a, dn_b), (up_a, b), (up_a, dn_b))[j]
         return copy(back7_send.at[j], back7_recv.at[j], back7_send_sem.at[j], back7_recv_sem.at[j], peer)
 
-    def both(w, first_col):
-        return jnp.concatenate(
-            [pack(x_ref, 6 * w + 3, 6, first_col), pack(g_ref, 6 * w + 3, 6, first_col)], axis=0
-        ).astype(BF)
-
-    for w in range(7):
-        send[w] = both(w, 6 * (w % 2))
-        if w == 0:
-            pl.semaphore_wait(barrier, len(peers))
-        forth(w, (a, up_b) if w % 2 else (a, dn_b)).start()
+    loads[0].wait()
+    for w in range(2):
+        send[w, 0] = padded(pack(x_ref, 6 * w + 3, 6, 6 * (w % 2)))
+    loads[1].wait()
+    for w in range(2):
+        send[w, 1] = padded(pack(g_ref, 6 * w + 3, 6, 6 * (w % 2)))
+    pl.semaphore_wait(barrier, len(peers))
+    for k in range(2):
+        for w in range(2):
+            forth(w, k, (a, up_b) if w % 2 else (a, dn_b)).start()
+    for w in range(2, 7):
+        for k, ref in enumerate((x_ref, g_ref)):
+            send[w, k] = padded(pack(ref, 6 * w + 3, 6, 6 * (w % 2)))
+            forth(w, k, (a, up_b) if w % 2 else (a, dn_b)).start()
     for j, (first_row, first_col) in enumerate(((45, 6), (0, 0), (0, 6))):
         send7[j] = piece_of(pack(x_ref, first_row, 3, first_col), pack(g_ref, first_row, 3, first_col))
         forth7(j).start()
 
     for w in range(7):
-        own[w] = both(w, 6 - 6 * (w % 2))
-
+        for k, ref in enumerate((x_ref, g_ref)):
+            own[w, k] = padded(pack(ref, 6 * w + 3, 6, 6 - 6 * (w % 2)))
+
+    loads[2].wait()
+    loads[3].wait()
     w_qkv_t[...] = w_qkv[...].T
     w_out_t[...] = w_out[...].T
     head = lax.broadcasted_iota(jnp.int32, (KEYS, 256), 1) // 32
-    ones_big[...] = jnp.where(lax.broadcasted_iota(jnp.int32, (KEYS, 256), 0) // TOK == head, 1.0, 0.0).astype(BF)
+    place = key_head(lax.broadcasted_iota(jnp.int32, (KEYS, 256), 0))
+    ones_big[...] = jnp.where(place == head, 1.0, 0.0).astype(BF)
     head = lax.broadcasted_iota(jnp.int32, (256, KEYS), 0) // 32
-    ones_big_t[...] = jnp.where(lax.broadcasted_iota(jnp.int32, (256, KEYS), 1) // TOK == head, 1.0, 0.0).astype(BF)
+    place = key_head(lax.broadcasted_iota(jnp.int32, (256, KEYS), 1))
+    minus_ones_t[...] = jnp.where(place == head, -1.0, 0.0).astype(BF)
     head = lax.broadcasted_iota(jnp.int32, (256, 256), 1) // 32
     ones_blk[...] = jnp.where(lax.broadcasted_iota(jnp.int32, (256, 256), 0) // 32 == head, 1.0, 0.0).astype(BF)
     for half in range(2):
-        key_head = lax.broadcasted_iota(jnp.int32, (1, KEYS), 1) // TOK
+        col_head = key_head(lax.broadcasted_iota(jnp.int32, (1, KEYS), 1))
         lane_head = lax.broadcasted_iota(jnp.int32, (1, 256), 1) // 32
         keys = jnp.zeros((1, KEYS), F32)
         lanes = jnp.zeros((1, 256), F32)
         for h in range(8):
-            keys = jnp.where(key_head == h, scale_ref[half * 8 + h] * LOG2E, keys)
+            keys = jnp.where(col_head == h, scale_ref[half * 8 + h] * LOG2E, keys)
             lanes = jnp.where(lane_head == h, scale_ref[half * 8 + h], lanes)
         scale_cols[half : half + 1, :] = keys
         scale_lanes[half : half + 1, :] = lanes
 
+    def results(w, part, branch, dshifted):
+        at = part * TOK
+        if branch is not None:
+            own_res[w, 0:HALF] = branch[at : at + HALF].astype(BF)
+            back_send[w, 0:HALF] = branch[at + HALF : at + TOK].astype(BF)
+        if dshifted is not None:
+            own_res[w, 80 : 80 + HALF] = dshifted[at : at + HALF].astype(BF)
+            back_send[w, 80 : 80 + HALF] = dshifted[at + HALF : at + TOK].astype(BF)
+
+    for w in range(8):
+        for row in (HALF, 80 + HALF):
+            back_send[w, row : row + 8] = jnp.zeros((8, WIDTH), BF)
+
     @pl.loop(0, 4)
     def _(pair):
         w = 2 * pair
-        forth(w, (a, up_b)).wait_recv()
+        forth(w, 0, (a, up_b)).wait_recv()
 
         @pl.when(pair < 3)
         def _():
-            forth(w + 1, (a, up_b)).wait_recv()
+            forth(w + 1, 0, (a, up_b)).wait_recv()
 
         @pl.when(pair == 3)
         def _():
             for j in range(3):
                 forth7(j).wait_recv()
-            low_x, low_g = pack(x_ref, 45, 3, 0), pack(g_ref, 45, 3, 0)
-            side_x, side_g = unpiece(recv7[0])
-            down_x, down_g = unpiece(recv7[1])
-            diag_x, diag_g = unpiece(recv7[2])
-            own[7] = jnp.concatenate([low_x, down_x, low_g, down_g], axis=0).astype(BF)
-            recv[7] = jnp.concatenate([side_x, diag_x, side_g, diag_g], axis=0).astype(BF)
-
-        blocks = [ref[w + i].astype(F32) for i in range(2) for ref in (own, recv)]
-        xw = jnp.concatenate([block[:HALF] for block in blocks], axis=0).astype(BF)
-        gw = jnp.concatenate([block[HALF:] for block in blocks], axis=0)
+            low = pack(x_ref, 45, 3, 0), pack(g_ref, 45, 3, 0)
+            side, down, diag = (unpiece(recv7[j]) for j in range(3))
+            for k in range(2):
+                own[7, k] = padded(jnp.concatenate([low[k], down[k]], axis=0))
+                recv[7, k] = padded(jnp.concatenate([side[k], diag[k]], axis=0))
+
+        def tokens(k):
+            blocks = [ref[w + i, k].astype(F32)[:HALF] for i in range(2) for ref in (own, recv)]
+            return jnp.concatenate(blocks, axis=0)
+
+        def wait_gw():
+            forth(w, 1, (a, up_b)).wait_recv()
+
+            @pl.when(pair < 3)
+            def _():
+                forth(w + 1, 1, (a, up_b)).wait_recv()
+
+            return tokens(1)
+
+        xw = tokens(0).astype(BF)
         split = jnp.logical_and(pair == 3, a == n_lat - 1)
-        branch, dshifted, att, dproj, dqkv = pair_math(
+        branch, att, dproj, dqkv = pair_math(
             xw,
-            gw,
+            wait_gw,
             split,
             w_qkv,
-            w_qkv_t,
             w_out,
             w_out_t,
             gain_ref[...],
             scale_cols,
             scale_lanes,
             ones_big,
-            ones_big_t,
+            minus_ones_t,
             ones_blk,
         )
         for i in range(2):
-            at = i * TOK
-            own_res[w + i] = jnp.concatenate(
-                [branch[at : at + HALF], dshifted[at : at + HALF]], axis=0
-            ).astype(BF)
-            back_send[w + i] = jnp.concatenate(
-                [branch[at + HALF : at + TOK], dshifted[at + HALF : at + TOK]], axis=0
-            ).astype(BF)
-        back(w, (a, up_b)).start()
-
-        @pl.when(pair < 3)
-        def _():
-            back(w + 1, (a, dn_b)).start()
-
+            results(w + i, i, branch, None)
         rows = pl.ds(pl.multiple_of(pair * 2 * TOK, 2 * TOK), 2 * TOK)
         x_all[rows, :] = xw
         att_all[rows, :] = att
         dproj_all[rows, :] = dproj
         dqkv_all[rows, :] = dqkv
 
-    ours = own_res[7].astype(F32)
-    theirs = back_send[7].astype(F32)
-    back7_send[0] = piece_of(theirs[:QUART], theirs[HALF : HALF + QUART])
-    back7_send[1] = piece_of(ours[QUART:HALF], ours[HALF + QUART :])
-    back7_send[2] = piece_of(theirs[QUART:HALF], theirs[HALF + QUART :])
-    for j in range(3):
-        back7(j).start()
-
-    @pl.loop(0, 2)
-    def _(side):
-        owner = core * side + (1 - core) * (1 - side)
+        @pl.when(pair < 3)
+        def _():
+            dshifted = nn(dqkv_all[rows, :], w_qkv_t[...])
+            for i in range(2):
+                results(w + i, i, None, dshifted)
+            back(w, (a, up_b)).start()
+            back(w + 1, (a, dn_b)).start()
+
+    def columns_of(owner, side):
         at = pl.multiple_of(owner * 768, 256)
         chunks = [tn(x_all[...], dqkv_all[:, pl.ds(at + i * 256, 256)]) for i in range(3)]
         chunks.append(tn(dproj_all[...], att_all[:, pl.ds(pl.multiple_of(owner * 256, 256), 256)]))
@@ -388,6 +448,8 @@
                 vv = yy * (1 - owner) + xx * owner
                 grads[side, uu, vv, zz] = joined[lon]
 
+    columns_of(1 - core, 0)
+
     order = (2, 1, 3, 0)
     pairs = []
     for i, step in enumerate(order):
@@ -395,6 +457,19 @@
         c.start()
         pairs.append(c)
 
+    columns_of(core, 1)
+    dshifted = nn(dqkv_all[6 * TOK :, :], w_qkv_t[...])
+    for i in range(2):
+        results(6 + i, i, None, dshifted)
+    back(6, (a, up_b)).start()
+    ours = own_res[7].astype(F32)
+    theirs = back_send[7].astype(F32)
+    back7_send[0] = piece_of(theirs[:QUART], theirs[80 : 80 + QUART])
+    back7_send[1] = piece_of(ours[QUART:HALF], ours[80 + QUART : 80 + HALF])
+    back7_send[2] = piece_of(theirs[QUART:HALF], theirs[80 + QUART : 80 + HALF])
+    for j in range(3):
+        back7(j).start()
+
     def add_pair(i):
         pairs[i].wait_recv()
         chunk = mod(u + order[i], 4)
@@ -406,7 +481,7 @@
     def halves_of(w, left):
         came = (w % 2 == 0) == left
         block = (back_recv if came else own_res)[w].astype(F32)
-        return block[:HALF], block[HALF:]
+        return block[:HALF], block[80 : 80 + HALF]
 
     def assemble(lev, left, tops, lows):
         parts = [halves_of(w, left) for w in range(7)]
@@ -420,6 +495,14 @@
                 )
                 cc = c if left else c + 6
                 dst[lev, cc] = (ref[lev, cc].astype(F32) + jnp.concatenate(strip, axis=0)).astype(BF)
+        place = pl.ds(0 if left else 6, 6)
+        for k, (src, dst) in enumerate(((out_ref, out_hbm), (gin_ref, gin_hbm))):
+            i = (2 * lev + (0 if left else 1)) * 2 + k
+            c = pltpu.make_async_copy(src.at[lev, place], dst.at[lev, place], store_sem.at[i])
+            c.start()
+            stores.append(c)
+
+    stores = []
 
     add_pair(0)
     relay_up = copy(mine.at[0, pl.ds(0, 2)], ring_relay.at[0], relay_send_sem.at[0], relay_recv_sem.at[0], nxt)
@@ -455,7 +538,7 @@
     for j in range(3):
         back7(j).wait_recv()
     block = own_res[7].astype(F32)
-    near = (block[:QUART], block[HALF : HALF + QUART])
+    near = (block[:QUART], block[80 : 80 + QUART])
     side, down, diag = (unpiece(back7_recv[j]) for j in range(3))
     assemble(0, True, down, near)
     assemble(0, False, diag, side)
@@ -502,7 +585,8 @@
         gathers.append(c)
 
     for w in range(7):
-        forth(w, (a, up_b)).wait_send()
+        for k in range(2):
+            forth(w, k, (a, up_b)).wait_send()
         back(w, (a, up_b)).wait_send()
     for j in range(3):
         forth7(j).wait_send()
@@ -519,13 +603,35 @@
         go_ref[:, owner * 256 : owner * 256 + 256] = whole[2 * owner + 1, 8:16, :]
     for c in gathers:
         c.wait_send()
+    for c in stores:
+        c.wait()
+
+
+def move_kernel(*refs):
+    sources, targets, held, in_sem, out_sem = refs[:4], refs[4:8], refs[8:12], refs[12], refs[13]
+    moves = []
+    for i in range(4):
+        for part in range(2) if i < 2 else (0,):
+            n = len(moves)
+            views = [ref.at[part] if i < 2 else ref for ref in (sources[i], held[i], targets[i])]
+            first = pltpu.make_async_copy(views[0], views[1], in_sem.at[n])
+            second = pltpu.make_async_copy(views[1], views[2], out_sem.at[n])
+            first.start()
+            moves.append((first, second))
+    for first, second in moves:
+        first.wait()
+        second.start()
+    for first, second in moves:
+        second.wait()
 
 
 def body(inputs, cotangent, w_qkv, w_out, gain, logit_scale):
     vmem = pl.BlockSpec(memory_space=pltpu.VMEM)
     smem = pl.BlockSpec(memory_space=pltpu.SMEM)
     dma = pltpu.SemaphoreType.DMA
-    blocks = pltpu.VMEM((8, TOK, WIDTH), BF)
+    anywhere = pl.BlockSpec(memory_space=pl.ANY)
+    halves = pltpu.VMEM((8, 2, 80, WIDTH), BF)
+    blocks = pltpu.VMEM((8, 160, WIDTH), BF)
     pieces = pltpu.VMEM((3, 80, WIDTH), BF)
     x_view = inputs.transpose(0, 2, 1, 3)
     g_view = cotangent.transpose(0, 2, 1, 3)
@@ -537,9 +643,18 @@
             jax.ShapeDtypeStruct((8, 3 * WIDTH), F32),
             jax.ShapeDtypeStruct((8, WIDTH), F32),
         ],
-        in_specs=[vmem] * 5 + [smem],
-        out_specs=[vmem] * 4,
-        scratch_shapes=[blocks] * 6
+        in_specs=[anywhere] * 4 + [vmem, smem],
+        out_specs=[anywhere] * 2 + [vmem] * 2,
+        scratch_shapes=[
+            pltpu.VMEM(x_view.shape, BF),
+            pltpu.VMEM(x_view.shape, BF),
+            pltpu.VMEM(w_qkv.shape, BF),
+            pltpu.VMEM(w_out.shape, BF),
+            pltpu.VMEM(x_view.shape, BF),
+            pltpu.VMEM(x_view.shape, BF),
+        ]
+        + [halves] * 3
+        + [blocks] * 3
         + [pieces] * 4
         + [
             pltpu.VMEM((8 * TOK, WIDTH), BF),
@@ -565,18 +680,28 @@
             pltpu.VMEM((16, 256), F32),
             pltpu.VMEM((4, 16, 256), F32),
         ]
-        + [dma((7,))] * 4
+        + [dma((7, 2))] * 2
+        + [dma((7,))] * 2
         + [dma((3,))] * 4
         + [dma((4,))] * 2
         + [dma((2,))] * 2
         + [dma((4,))] * 2
         + [dma((3,))] * 2
         + [dma((7,))] * 2
-        + [dma((3,))] * 2,
+        + [dma((3,))] * 2
+        + [dma((4,)), dma((8,))],
         compiler_params=pltpu.CompilerParams(
             collective_id=0, has_side_effects=True, vmem_limit_bytes=56 * 2**20
         ),
     )(x_view, g_view, w_qkv, w_out, gain.reshape(1, WIDTH), logit_scale)
+    results = (out, grad_in, share_qkv, share_out)
+    out, grad_in, share_qkv, share_out = pl.pallas_call(
+        move_kernel,
+        out_shape=[jax.ShapeDtypeStruct(r.shape, r.dtype) for r in results],
+        in_specs=[anywhere] * 4,
+        out_specs=[anywhere] * 4,
+        scratch_shapes=[pltpu.VMEM(r.shape, r.dtype) for r in results] + [dma((6,)), dma((6,))],
+    )(*results)
     return out.transpose(0, 2, 1, 3), grad_in.transpose(0, 2, 1, 3), share_qkv, share_out.T
 
 

time: 82.6 us -> 76.4 us (0.925)
  local copies, waits for them, and re-layouts: 4.71 us -> 0 us
  Pallas kernels: 77.2 us -> 75.5 us
    unnamed x10 -> x0, local copies, waits for them, and re-layouts: 4.71 us -> none
    pallas_call x1, Pallas kernels: 77.2 us -> 72.9 us  [body(): pl.pallas_call(block_kernel, out_shape=[jax.ShapeDtypeStruct(x_view.shape...]
    pallas_call x0 -> x1, Pallas kernels: none -> 2.57 us  [body(): pl.pallas_call(move_kernel, out_shape=[jax.ShapeDtypeStruct(r.shape, r.dt...]
where the time goes in v3:
time: 76.4 us; the launch traced here: 76.3 us
  Pallas kernels  75.5 us (99%)
  between operations  0.8 us (1%)
    pallas_call x1, Pallas kernels, body(): pl.pallas_call(block_kernel, out_shape=[jax.ShapeDtypeStruct(x_view.shape...  72.9 us
    pallas_call x1, Pallas kernels, body(): pl.pallas_call(move_kernel, out_shape=[jax.ShapeDtypeStruct(r.shape, r.dt...  2.57 us

profile of v3, /device:TPU:1, one launch (start us, length us, event | category | flops | bytes accessed | tf_op | source)
XLA Modules:
  0.0 76.3 jit_solution(13037798600332681484)
XLA Ops:
  0.6 72.9 %shard_map.93 = (bf16[2,12,48,512]{3,2,1,0:T(8,128)(2,1)}, bf16[2,12,48,512]{3,2,1,0:T(8,128)(2,1)}, f32[8,1536]{1,0:T(8,128)}, f32[8,512]{1,0:T(8,128)}) custom-call(bf16[2,12,48,512]{3,2,1,0:T(8,128)(2,1)} %bitcast.6, bf16[2,12,48,512]{3,2,1,0:T(8,128)(2,1)} %bitcast.7, bf16[512,1536]{1,0:T(8,128)(2,1)} %w_qkv_hbm.1, bf16[512,512]{1,0:T(8,128)(2,1)} %w_out_hbm.1, ...), custom_call_target="tpu_custom_call" | custom-call | tf_op jit(solution)/shard_map/pallas_call | solution.py:638
  73.5 2.6 %shard_map.94 = (bf16[2,12,48,512]{3,2,1,0:T(8,128)(2,1)}, bf16[2,12,48,512]{3,2,1,0:T(8,128)(2,1)}, f32[8,1536]{1,0:T(8,128)}, f32[8,512]{1,0:T(8,128)}) custom-call(bf16[2,12,48,512]{3,2,1,0:T(8,128)(2,1)} %get-tuple-element.12.refs_0_, bf16[2,12,48,512]{3,2,1,0:T(8,128)(2,1)} %get-tuple-element.13.refs_1_, f32[8,1536]{1,0:T(8,128)} %get-tuple-element.14.refs_2_, ...), custom_call_target="tpu_custom_call" | custom-call | tf_op jit(solution)/shard_map/pallas_call | solution.py:698

commit v4 on v3

--- a/solution.py
+++ b/solution.py
@@ -39,32 +39,36 @@
     return jnp.where(place < 1024, place % 128, 128 + (place - 1024) % 16)
 
 
-def spread(part):
-    head = lax.broadcasted_iota(jnp.int32, part.shape, 1) // 32
+def alone(part, axis, heads):
+    head = lax.broadcasted_iota(jnp.int32, part.shape, axis) // 32
     zero = jnp.zeros_like(part)
-    alone = [jnp.where(head == h, part, zero) for h in range(8)]
-    return jnp.concatenate([one[:128] for one in alone] + [one[128:] for one in alone], axis=0)
-
-
-def spread_t(part):
-    main = part[:128].T
-    row = lax.broadcasted_iota(jnp.int32, main.shape, 0) // 32
-    zero = jnp.zeros_like(main)
-    rest = part[128:]
-    head = lax.broadcasted_iota(jnp.int32, rest.shape, 1) // 32
-    last = jnp.concatenate([jnp.where(head == h, rest, jnp.zeros_like(rest)) for h in range(8)], axis=0).T
-    return jnp.concatenate([jnp.where(row == h, main, zero) for h in range(8)] + [last], axis=1)
-
-
-def pick(full):
-    def choose(first, step, rows):
-        head = lax.broadcasted_iota(jnp.int32, (rows, 256), 1) // 32
-        chosen = full[first : first + rows]
-        for h in range(1, 8):
-            chosen = jnp.where(head == h, full[first + step * h : first + step * h + rows], chosen)
-        return chosen
-
-    return jnp.concatenate([choose(0, 128, 128), choose(1024, 16, 16)], axis=0)
+    return [jnp.where(head == h, part, zero) for h in range(heads)]
+
+
+def rows4(part, p):
+    return jnp.concatenate(alone(part[:128, 128 * p : 128 * p + 128], 1, 4), axis=0)
+
+
+def rows_last(part):
+    return jnp.concatenate(alone(part[128:], 1, 8), axis=0)
+
+
+def cols4(main_t, p):
+    return jnp.concatenate(alone(main_t[128 * p : 128 * p + 128], 0, 4), axis=1)
+
+
+def by_keys(e, d):
+    d_t = d.T
+    blocks = []
+    for p in range(4):
+        two = nn(d_t[64 * p : 64 * p + 64], e[:, 256 * p : 256 * p + 256])
+        blocks += [two[:32, :128], two[32:, 128:]]
+    full = tn(e[:, 1024:], d)
+    head = lax.broadcasted_iota(jnp.int32, (16, 256), 1) // 32
+    last = full[:16]
+    for h in range(1, 8):
+        last = jnp.where(head == h, full[16 * h : 16 * h + 16], last)
+    return jnp.concatenate([jnp.concatenate(blocks, axis=0).T, last], axis=0)
 
 
 def head_sum(value, ones_block):
@@ -77,8 +81,10 @@
     return nn(high, ones_block) + nn(low, ones_block)
 
 
-def pair_math(x, wait_gw, split, w_qkv, w_out, w_out_t, gain, scale_cols, scale_lanes, ones_big, minus_ones_t, ones_blk):
+def pair_math(x, hand_over, split, w_qkv, w_out, w_out_t, gain, scale_cols, scale_lanes, ones_big, minus_ones_t, ones_blk):
     ones_block = ones_blk[...]
+    ones4, ones_last = ones_big[0:512, 0:128], ones_big[1024:, :]
+    minus4, minus_last = minus_ones_t[0:128, 0:512], minus_ones_t[:, 1024:]
     qkv = nn(x, w_qkv[...]).astype(BF)
     row = lax.broadcasted_iota(jnp.int32, (TOK, 1), 0)
     col = key_token(lax.broadcasted_iota(jnp.int32, (1, KEYS), 1))
@@ -102,24 +108,30 @@
         for half in range(2):
             lo = half * 256
             uq, uk = vec[half][6][r], vec[half][7][r]
-            k_big = spread(uk)
             v = qkv[r, 1024 + lo : 1280 + lo]
-            v_big = spread(v)
-            e = jnp.exp2(nn(uq, spread_t(uk)) * scale_cols[half : half + 1, :])
+            k_t = uk[:128].T
+            scores = [nn(uq[:, 128 * p : 128 * p + 128], cols4(k_t, p)) for p in range(2)]
+            scores.append(nn(uq, rows_last(uk).T))
+            e = jnp.exp2(jnp.concatenate(scores, axis=1) * scale_cols[half : half + 1, :])
             if g == 1:
                 e = jnp.where(allowed, e, 0.0)
             e = e.astype(BF)
-            both = nn(e, jnp.concatenate([v_big, ones_big[...]], axis=1))
-            r_den = 1.0 / both[:, 256:]
-            att[g][half] = (both[:, :256] * r_den).astype(BF)
-            saved[g, half] = (k_big, v, e, r_den, uq)
+            v_last = rows_last(v)
+            last = nn(e[:, 1024:], jnp.concatenate([v_last, ones_last], axis=1))
+            main = [
+                nn(e[:, 512 * p : 512 * p + 512], jnp.concatenate([rows4(v, p), ones4], axis=1)) for p in range(2)
+            ]
+            num = jnp.concatenate([one[:, :128] for one in main], axis=1) + last[:, :256]
+            r_den = 1.0 / (jnp.concatenate([one[:, 128:] for one in main], axis=1) + last[:, 256:])
+            att[g][half] = (num * r_den).astype(BF)
+            saved[g, half] = (v, v_last, e, r_den, uq, uk)
     att_b = jnp.concatenate([jnp.concatenate(one, axis=1) for one in att], axis=0)
     proj = nn(att_b, w_out[...])
     dev = proj - jnp.mean(proj, -1, keepdims=True)
     inv = lax.rsqrt(jnp.mean(dev * dev, -1, keepdims=True) + EPS)
     normed = dev * inv
     branch = gain * normed
-    up = gain * wait_gw()
+    up = gain * hand_over(branch)
     dproj = (
         (up - jnp.mean(up, -1, keepdims=True) - normed * jnp.mean(up * normed, -1, keepdims=True))
         * inv
@@ -130,19 +142,30 @@
         r = slice(g * TOK, (g + 1) * TOK)
         for half in range(2):
             lo = half * 256
-            k_big, v, e, r_den, uq = saved[g, half]
+            v, v_last, e, r_den, uq, uk = saved[g, half]
             dh = datt[r, lo : lo + 256].astype(F32) * r_den
             dh_b = dh.astype(BF)
             dd = (dh * att[g][half].astype(F32)).astype(BF)
-            t = nn(
-                jnp.concatenate([dh_b, dd], axis=1),
-                jnp.concatenate([spread_t(v), minus_ones_t[...]], axis=0),
+            v_t = v[:128].T
+            t = []
+            for p in range(2):
+                lanes = slice(128 * p, 128 * p + 128)
+                t.append(
+                    nn(
+                        jnp.concatenate([dh_b[:, lanes], dd[:, lanes]], axis=1),
+                        jnp.concatenate([cols4(v_t, p), minus4], axis=0),
+                    )
+                )
+            t.append(
+                nn(jnp.concatenate([dh_b, dd], axis=1), jnp.concatenate([v_last.T, minus_last], axis=0))
             )
+            t = jnp.concatenate(t, axis=1)
             ds = (e.astype(F32) * t).astype(BF)
             lanes = scale_lanes[half : half + 1, :]
-            dq[g, half] = nn(ds, k_big) * lanes
-            dk[g, half] = pick(tn(ds, uq)) * lanes
-            dv[g, half] = pick(tn(e, dh_b)).astype(BF)
+            duq = [nn(ds[:, 512 * p : 512 * p + 512], rows4(uk, p)) for p in range(2)]
+            dq[g, half] = (jnp.concatenate(duq, axis=1) + nn(ds[:, 1024:], rows_last(uk))) * lanes
+            dk[g, half] = by_keys(ds, uq) * lanes
+            dv[g, half] = by_keys(e, dh_b).astype(BF)
     cols = [None] * 6
     for half in range(2):
         q_len, k_len, q_inv, k_inv, uq, uk, _, _ = vec[half]
@@ -154,7 +177,7 @@
         cols[2 + half] = ((duk - k_tail) * k_inv).astype(BF)
         cols[4 + half] = jnp.concatenate([dv[0, half], dv[1, half]], axis=0)
     dqkv = jnp.concatenate(cols, axis=1)
-    return branch, att_b, dproj, dqkv
+    return att_b, dproj, dqkv
 
 
 def pack(ref, first_row, rows, first_col):
@@ -302,16 +325,18 @@
     def forth(w, k, peer):
         return copy(send.at[w, k], recv.at[w, k], send_sem.at[w, k], recv_sem.at[w, k], peer)
 
-    def back(w, peer):
-        return copy(back_send.at[w], back_recv.at[w], back_send_sem.at[w], back_recv_sem.at[w], peer)
+    def back(w, k, peer):
+        return copy(back_send.at[w, k], back_recv.at[w, k], back_send_sem.at[w, k], back_recv_sem.at[w, k], peer)
 
     def forth7(j):
         peer = ((a, up_b), (dn_a, b), (dn_a, up_b))[j]
         return copy(send7.at[j], recv7.at[j], send7_sem.at[j], recv7_sem.at[j], peer)
 
-    def back7(j):
+    def back7(j, k):
         peer = ((a, dn_b), (up_a, b), (up_a, dn_b))[j]
-        return copy(back7_send.at[j], back7_recv.at[j], back7_send_sem.at[j], back7_recv_sem.at[j], peer)
+        return copy(
+            back7_send.at[j, k], back7_recv.at[j, k], back7_send_sem.at[j, k], back7_recv_sem.at[j, k], peer
+        )
 
     loads[0].wait()
     for w in range(2):
@@ -358,18 +383,22 @@
         scale_cols[half : half + 1, :] = keys
         scale_lanes[half : half + 1, :] = lanes
 
-    def results(w, part, branch, dshifted):
+    def results(w, part, k, values):
         at = part * TOK
-        if branch is not None:
-            own_res[w, 0:HALF] = branch[at : at + HALF].astype(BF)
-            back_send[w, 0:HALF] = branch[at + HALF : at + TOK].astype(BF)
-        if dshifted is not None:
-            own_res[w, 80 : 80 + HALF] = dshifted[at : at + HALF].astype(BF)
-            back_send[w, 80 : 80 + HALF] = dshifted[at + HALF : at + TOK].astype(BF)
+        own_res[w, k, 0:HALF] = values[at : at + HALF].astype(BF)
+        back_send[w, k, 0:HALF] = values[at + HALF : at + TOK].astype(BF)
+
+    def send_back7(k):
+        ours = own_res[7, k].astype(F32)
+        theirs = back_send[7, k].astype(F32)
+        pad = jnp.zeros((48 - QUART, WIDTH), F32)
+        for j, quarter in enumerate((theirs[:QUART], ours[QUART:HALF], theirs[QUART:HALF])):
+            back7_send[j, k] = jnp.concatenate([quarter, pad], axis=0).astype(BF)
+            back7(j, k).start()
 
     for w in range(8):
-        for row in (HALF, 80 + HALF):
-            back_send[w, row : row + 8] = jnp.zeros((8, WIDTH), BF)
+        for k in range(2):
+            back_send[w, k, HALF:] = jnp.zeros((8, WIDTH), BF)
 
     @pl.loop(0, 4)
     def _(pair):
@@ -394,20 +423,28 @@
             blocks = [ref[w + i, k].astype(F32)[:HALF] for i in range(2) for ref in (own, recv)]
             return jnp.concatenate(blocks, axis=0)
 
-        def wait_gw():
+        def hand_over(branch):
+            for i in range(2):
+                results(w + i, i, 0, branch)
+            back(w, 0, (a, up_b)).start()
             forth(w, 1, (a, up_b)).wait_recv()
 
             @pl.when(pair < 3)
             def _():
+                back(w + 1, 0, (a, dn_b)).start()
                 forth(w + 1, 1, (a, up_b)).wait_recv()
+
+            @pl.when(pair == 3)
+            def _():
+                send_back7(0)
 
             return tokens(1)
 
         xw = tokens(0).astype(BF)
         split = jnp.logical_and(pair == 3, a == n_lat - 1)
-        branch, att, dproj, dqkv = pair_math(
+        att, dproj, dqkv = pair_math(
             xw,
-            wait_gw,
+            hand_over,
             split,
             w_qkv,
             w_out,
@@ -419,25 +456,27 @@
             minus_ones_t,
             ones_blk,
         )
-        for i in range(2):
-            results(w + i, i, branch, None)
         rows = pl.ds(pl.multiple_of(pair * 2 * TOK, 2 * TOK), 2 * TOK)
         x_all[rows, :] = xw
         att_all[rows, :] = att
         dproj_all[rows, :] = dproj
         dqkv_all[rows, :] = dqkv
 
+        dshifted = nn(dqkv, w_qkv_t[...])
+        for i in range(2):
+            results(w + i, i, 1, dshifted)
+        back(w, 1, (a, up_b)).start()
+
         @pl.when(pair < 3)
         def _():
-            dshifted = nn(dqkv_all[rows, :], w_qkv_t[...])
-            for i in range(2):
-                results(w + i, i, None, dshifted)
-            back(w, (a, up_b)).start()
-            back(w + 1, (a, dn_b)).start()
+            back(w + 1, 1, (a, dn_b)).start()
+
+    send_back7(1)
 
     def columns_of(owner, side):
         at = pl.multiple_of(owner * 768, 256)
-        chunks = [tn(x_all[...], dqkv_all[:, pl.ds(at + i * 256, 256)]) for i in range(3)]
+        wide = tn(x_all[...], dqkv_all[:, pl.ds(at, 768)])
+        chunks = [wide[:, i * 256 : (i + 1) * 256] for i in range(3)]
         chunks.append(tn(dproj_all[...], att_all[:, pl.ds(pl.multiple_of(owner * 256, 256), 256)]))
         for low in range(2):
             halves = [chunk.reshape(64, 8, 256) for chunk in chunks[2 * low : 2 * low + 2]]
@@ -458,17 +497,6 @@
         pairs.append(c)
 
     columns_of(core, 1)
-    dshifted = nn(dqkv_all[6 * TOK :, :], w_qkv_t[...])
-    for i in range(2):
-        results(6 + i, i, None, dshifted)
-    back(6, (a, up_b)).start()
-    ours = own_res[7].astype(F32)
-    theirs = back_send[7].astype(F32)
-    back7_send[0] = piece_of(theirs[:QUART], theirs[80 : 80 + QUART])
-    back7_send[1] = piece_of(ours[QUART:HALF], ours[80 + QUART : 80 + HALF])
-    back7_send[2] = piece_of(theirs[QUART:HALF], theirs[80 + QUART : 80 + HALF])
-    for j in range(3):
-        back7(j).start()
 
     def add_pair(i):
         pairs[i].wait_recv()
@@ -478,29 +506,32 @@
         def _(vv):
             mine[i, vv] = (grads[1, chunk, vv].astype(F32) + pair_recv[i, vv].astype(F32)).astype(BF)
 
-    def halves_of(w, left):
-        came = (w % 2 == 0) == left
-        block = (back_recv if came else own_res)[w].astype(F32)
-        return block[:HALF], block[80 : 80 + HALF]
-
-    def assemble(lev, left, tops, lows):
-        parts = [halves_of(w, left) for w in range(7)]
+    def assemble(k, lev, left):
+        parts = []
+        for w in range(7):
+            came = (w % 2 == 0) == left
+            parts.append((back_recv if came else own_res)[w, k].astype(F32))
+        top = back7_recv[1 if left else 2, k].astype(F32)
+        low = (own_res[7, k] if left else back7_recv[0, k]).astype(F32)
+        ref, dst, hbm = ((x_ref, out_ref, out_hbm), (g_ref, gin_ref, gin_hbm))[k]
         for c in range(6):
             at = lev * 6 + c
-            for k, (ref, dst) in enumerate(((x_ref, out_ref), (g_ref, gin_ref))):
-                strip = (
-                    [tops[k][at * 3 : at * 3 + 3]]
-                    + [one[k][at * 6 : at * 6 + 6] for one in parts]
-                    + [lows[k][at * 3 : at * 3 + 3]]
-                )
-                cc = c if left else c + 6
-                dst[lev, cc] = (ref[lev, cc].astype(F32) + jnp.concatenate(strip, axis=0)).astype(BF)
+            strip = (
+                [top[at * 3 : at * 3 + 3]] + [one[at * 6 : at * 6 + 6] for one in parts] + [low[at * 3 : at * 3 + 3]]
+            )
+            cc = c if left else c + 6
+            dst[lev, cc] = (ref[lev, cc].astype(F32) + jnp.concatenate(strip, axis=0)).astype(BF)
         place = pl.ds(0 if left else 6, 6)
-        for k, (src, dst) in enumerate(((out_ref, out_hbm), (gin_ref, gin_hbm))):
-            i = (2 * lev + (0 if left else 1)) * 2 + k
-            c = pltpu.make_async_copy(src.at[lev, place], dst.at[lev, place], store_sem.at[i])
-            c.start()
-            stores.append(c)
+        i = (2 * lev + (0 if left else 1)) * 2 + k
+        c = pltpu.make_async_copy(dst.at[lev, place], hbm.at[lev, place], store_sem.at[i])
+        c.start()
+        stores.append(c)
+
+    def wait_back(k):
+        for w in range(7):
+            back(w, k, (a, up_b)).wait_recv()
+        for j in range(3):
+            back7(j, k).wait_recv()
 
     stores = []
 
@@ -533,15 +564,9 @@
     ring_dn_b = copy(mine.at[2, pl.ds(2, 2)], ring_recv.at[1, pl.ds(2, 2)], ring_send_sem.at[3], ring_recv_sem.at[3], prv)
     ring_dn_b.start()
 
-    for w in range(7):
-        back(w, (a, up_b)).wait_recv()
-    for j in range(3):
-        back7(j).wait_recv()
-    block = own_res[7].astype(F32)
-    near = (block[:QUART], block[80 : 80 + QUART])
-    side, down, diag = (unpiece(back7_recv[j]) for j in range(3))
-    assemble(0, True, down, near)
-    assemble(0, False, diag, side)
+    wait_back(0)
+    assemble(0, 0, True)
+    assemble(0, 0, False)
 
     for c in (ring_up_b, ring_dn_a, ring_up_a, ring_dn_b):
         c.wait_recv()
@@ -557,7 +582,7 @@
         c = copy(cut.at[mod(v + i + 1, 4)], line_recv.at[i], line_send_sem.at[i], line_recv_sem.at[i], line[i])
         c.start()
         lines.append(c)
-    assemble(1, True, down, near)
+    assemble(0, 1, True)
     for c in lines:
         c.wait_recv()
     piece[...] = (
@@ -568,7 +593,7 @@
         c = copy(piece.at[mod(z + i + 1, 8)], z_recv.at[i], z_send_sem.at[i], z_recv_sem.at[i], column[i])
         c.start()
         columns.append(c)
-    assemble(1, False, diag, side)
+    assemble(0, 1, False)
     for c in columns:
         c.wait_recv()
     total = piece[z].astype(F32)
@@ -584,13 +609,19 @@
         c.start()
         gathers.append(c)
 
+    wait_back(1)
+    for lev in range(2):
+        for left in (True, False):
+            assemble(1, lev, left)
+
     for w in range(7):
         for k in range(2):
             forth(w, k, (a, up_b)).wait_send()
-        back(w, (a, up_b)).wait_send()
+            back(w, k, (a, up_b)).wait_send()
     for j in range(3):
         forth7(j).wait_send()
-        back7(j).wait_send()
+        for k in range(2):
+            back7(j, k).wait_send()
     for c in pairs + [relay_up, relay_dn, ring_up_b, ring_dn_a, ring_up_a, ring_dn_b] + lines + columns:
         c.wait_send()
     for c in gathers:
@@ -631,8 +662,8 @@
     dma = pltpu.SemaphoreType.DMA
     anywhere = pl.BlockSpec(memory_space=pl.ANY)
     halves = pltpu.VMEM((8, 2, 80, WIDTH), BF)
-    blocks = pltpu.VMEM((8, 160, WIDTH), BF)
     pieces = pltpu.VMEM((3, 80, WIDTH), BF)
+    quarters = pltpu.VMEM((3, 2, 48, WIDTH), BF)
     x_view = inputs.transpose(0, 2, 1, 3)
     g_view = cotangent.transpose(0, 2, 1, 3)
     out, grad_in, share_qkv, share_out = pl.pallas_call(
@@ -653,9 +684,9 @@
             pltpu.VMEM(x_view.shape, BF),
             pltpu.VMEM(x_view.shape, BF),
         ]
-        + [halves] * 3
-        + [blocks] * 3
-        + [pieces] * 4
+        + [halves] * 6
+        + [pieces] * 2
+        + [quarters] * 2
         + [
             pltpu.VMEM((8 * TOK, WIDTH), BF),
             pltpu.VMEM((8 * TOK, WIDTH), BF),
@@ -680,9 +711,9 @@
             pltpu.VMEM((16, 256), F32),
             pltpu.VMEM((4, 16, 256), F32),
         ]
-        + [dma((7, 2))] * 2
-        + [dma((7,))] * 2
-        + [dma((3,))] * 4
+        + [dma((7, 2))] * 4
+        + [dma((3,))] * 2
+        + [dma((3, 2))] * 2
         + [dma((4,))] * 2
         + [dma((2,))] * 2
         + [dma((4,))] * 2

time: 76.4 us -> 74.6 us (0.976); the launches traced: 76.3 us -> 73.6 us
  Pallas kernels: 75.5 us -> 73 us
    pallas_call x1, Pallas kernels: 72.9 us -> 70.4 us  [body(): pl.pallas_call(block_kernel, out_shape=[jax.ShapeDtypeStruct(x_view.shape...]
where the time goes in v4:
time: 74.6 us; the launch traced here: 73.6 us
  Pallas kernels  73 us (98%)
    pallas_call x1, Pallas kernels, body(): pl.pallas_call(block_kernel, out_shape=[jax.ShapeDtypeStruct(x_view.shape...  70.4 us
    pallas_call x1, Pallas kernels, body(): pl.pallas_call(move_kernel, out_shape=[jax.ShapeDtypeStruct(r.shape, r.dt...  2.57 us

profile of v4, /device:TPU:1, one launch (start us, length us, event | category | flops | bytes accessed | tf_op | source)
XLA Modules:
  0.0 73.6 jit_solution(9459049501835283720)
XLA Ops:
  0.6 70.4 %shard_map.93 = (bf16[2,12,48,512]{3,2,1,0:T(8,128)(2,1)}, bf16[2,12,48,512]{3,2,1,0:T(8,128)(2,1)}, f32[8,1536]{1,0:T(8,128)}, f32[8,512]{1,0:T(8,128)}) custom-call(bf16[2,12,48,512]{3,2,1,0:T(8,128)(2,1)} %bitcast.6, bf16[2,12,48,512]{3,2,1,0:T(8,128)(2,1)} %bitcast.7, bf16[512,1536]{1,0:T(8,128)(2,1)} %w_qkv_hbm.1, bf16[512,512]{1,0:T(8,128)(2,1)} %w_out_hbm.1, ...), custom_call_target="tpu_custom_call" | custom-call | tf_op jit(solution)/shard_map/pallas_call | solution.py:669
  71.0 2.6 %shard_map.94 = (bf16[2,12,48,512]{3,2,1,0:T(8,128)(2,1)}, bf16[2,12,48,512]{3,2,1,0:T(8,128)(2,1)}, f32[8,1536]{1,0:T(8,128)}, f32[8,512]{1,0:T(8,128)}) custom-call(bf16[2,12,48,512]{3,2,1,0:T(8,128)(2,1)} %get-tuple-element.12.refs_0_, bf16[2,12,48,512]{3,2,1,0:T(8,128)(2,1)} %get-tuple-element.13.refs_1_, f32[8,1536]{1,0:T(8,128)} %get-tuple-element.14.refs_2_, ...), custom_call_target="tpu_custom_call" | custom-call | tf_op jit(solution)/shard_map/pallas_call | solution.py:729

commit v5 on v4

--- a/solution.py
+++ b/solution.py
@@ -385,8 +385,8 @@
 
     def results(w, part, k, values):
         at = part * TOK
-        own_res[w, k, 0:HALF] = values[at : at + HALF].astype(BF)
-        back_send[w, k, 0:HALF] = values[at + HALF : at + TOK].astype(BF)
+        own_res[w, k] = padded(values[at : at + HALF])
+        back_send[w, k] = padded(values[at + HALF : at + TOK])
 
     def send_back7(k):
         ours = own_res[7, k].astype(F32)
@@ -395,10 +395,6 @@
         for j, quarter in enumerate((theirs[:QUART], ours[QUART:HALF], theirs[QUART:HALF])):
             back7_send[j, k] = jnp.concatenate([quarter, pad], axis=0).astype(BF)
             back7(j, k).start()
-
-    for w in range(8):
-        for k in range(2):
-            back_send[w, k, HALF:] = jnp.zeros((8, WIDTH), BF)
 
     @pl.loop(0, 4)
     def _(pair):

time: 74.6 us -> 74.6 us (level)
  no operation moved by 1% of the time
where the time goes in v5:
time: 74.6 us; the launch traced here: 73.6 us
  Pallas kernels  73 us (98%)
    pallas_call x1, Pallas kernels, body(): pl.pallas_call(block_kernel, out_shape=[jax.ShapeDtypeStruct(x_view.shape...  70.4 us
    pallas_call x1, Pallas kernels, body(): pl.pallas_call(move_kernel, out_shape=[jax.ShapeDtypeStruct(r.shape, r.dt...  2.57 us

profile of v5, /device:TPU:1, one launch (start us, length us, event | category | flops | bytes accessed | tf_op | source)
XLA Modules:
  0.0 73.6 jit_solution(3504214686615780698)
XLA Ops:
  0.6 70.4 %shard_map.93 = (bf16[2,12,48,512]{3,2,1,0:T(8,128)(2,1)}, bf16[2,12,48,512]{3,2,1,0:T(8,128)(2,1)}, f32[8,1536]{1,0:T(8,128)}, f32[8,512]{1,0:T(8,128)}) custom-call(bf16[2,12,48,512]{3,2,1,0:T(8,128)(2,1)} %bitcast.6, bf16[2,12,48,512]{3,2,1,0:T(8,128)(2,1)} %bitcast.7, bf16[512,1536]{1,0:T(8,128)(2,1)} %w_qkv_hbm.1, bf16[512,512]{1,0:T(8,128)(2,1)} %w_out_hbm.1, ...), custom_call_target="tpu_custom_call" | custom-call | tf_op jit(solution)/shard_map/pallas_call | solution.py:665
  71.0 2.6 %shard_map.94 = (bf16[2,12,48,512]{3,2,1,0:T(8,128)(2,1)}, bf16[2,12,48,512]{3,2,1,0:T(8,128)(2,1)}, f32[8,1536]{1,0:T(8,128)}, f32[8,512]{1,0:T(8,128)}) custom-call(bf16[2,12,48,512]{3,2,1,0:T(8,128)(2,1)} %get-tuple-element.12.refs_0_, bf16[2,12,48,512]{3,2,1,0:T(8,128)(2,1)} %get-tuple-element.13.refs_1_, f32[8,1536]{1,0:T(8,128)} %get-tuple-element.14.refs_2_, ...), custom_call_target="tpu_custom_call" | custom-call | tf_op jit(solution)/shard_map/pallas_call | solution.py:725
